TPU v7x, 512 devices: a whole 4x4x16 slice. The times are simulated.
512 devices in a mesh: agent: 16 (over x, y), dp: 32 (over z, core).
Axes of the slice: x: 4, y: 4, z: 16, core: 2. Of those that a mesh axis runs over, the one named last changes fastest.
Arguments:
- learn_obs: bfloat16 [16, 1024, 16, 3456], P('agent', 'dp'), may hold values from -6 to 6
- own_obs: bfloat16 [16, 1024, 3456], P('agent', 'dp'), may hold values from -6 to 6
- opp_obs: bfloat16 [16, 1024, 3456], P('agent', 'dp'), may hold values from -6 to 6
- opponent: int32 [16, 1024, 1], P('agent', 'dp'), may hold values from 0 to 15; in each aligned block of 32 rows (0 to 31, 32 to 63, ..., all dimensions but the last counted through in order) at most 8 rows name the same one
- actions: int32 [16, 1024, 16], P('agent', 'dp'), may hold values from 0 to 17
- done: int32 [16, 1024, 16], P('agent', 'dp'), may hold values 0 or 1
- rewards: float32 [16, 1024, 16], P('agent', 'dp'), may hold values from -6 to 6
- behaviour: float32 [16, 1024, 16], P('agent', 'dp'), may hold values from -4.5 to -1.5
- core_master: float32 [16, 256, 3712], P('agent', 'dp'), may hold values from -0.109375 to 0.109375
- core_mom: float32 [16, 256, 3712], P('agent', 'dp'), may hold values from -6 to 6
- core_vel: float32 [16, 256, 3712], P('agent', 'dp'), may hold values from 0.1 to 1
- head_master: float32 [16, 19, 256], P('agent'), may hold values from -0.375 to 0.375
- head_mom: float32 [16, 19, 256], P('agent'), may hold values from -6 to 6
- head_vel: float32 [16, 19, 256], P('agent'), may hold values from 0.1 to 1
- rates: float32 [16], P('agent'), may hold values from 0.01 to 0.1
Outputs:
- own_logits: float32 [16, 1024, 18], P('agent', 'dp')
- opp_logits: bfloat16 [16, 1024, 18], P('agent', 'dp')
- new_core: float32 [16, 256, 3712], P('agent', 'dp')
- new_core_mom: float32 [16, 256, 3712], P('agent', 'dp')
- new_core_vel: float32 [16, 256, 3712], P('agent', 'dp')
- new_head: float32 [16, 19, 256], P('agent')
- new_head_mom: float32 [16, 19, 256], P('agent')
- new_head_vel: float32 [16, 19, 256], P('agent')
Inputs may be any that keep to these rules, and one draw needn't show every extreme that they name: Among the 32 environments of one device (aligned blocks of the environment dimension), at most 8 face the same opponent agent, and some device reaches 8 in every draw.
All inputs are finite; a program needn't handle non-finite values. No bound on the sum of `done` on one device may be relied on, other than what follows from the above.
Results may differ from a plain program's by a relative error of at most 0.023.
Values may be sent and summed in bfloat16 or wider, within the bound.
A program may use at most 64 MiB of HBM per device.

v0:
```python
import jax
import jax.numpy as jnp
from jax import lax
from jax.sharding import Mesh
from jax.sharding import PartitionSpec as P

BLOCK = 128
DP = ("dp_0", "dp_1")


gamma_rate = 0.99
baseline_cost = 0.5
entropy_cost = 0.05
beta_first = 0.9
beta_second = 0.99
adam_eps = 1e-08


def joined_along(blocks, dim):
    shape = list(blocks.shape[1:])
    shape[dim] *= blocks.shape[0]
    return jnp.moveaxis(blocks, 0, dim).reshape(shape)


def stacked_from(x, axes, order):
    blocks = x[None]
    for k in order:
        blocks = lax.all_gather(blocks, axes[k], axis=0, tiled=True)
    current = [lax.axis_size(axes[k]) for k in reversed(order)]
    blocks = blocks.reshape(*current, *x.shape)
    turned = sorted(range(len(order)), key=lambda place: order[len(order) - 1 - place])
    return blocks.transpose(*turned, *range(len(order), blocks.ndim)).reshape(-1, *x.shape)


def gather_axes(x, axes, order, dim):
    return joined_along(stacked_from(x, axes, order), dim)


def reduced_to_own(blocks, axes, order):
    shape = [lax.axis_size(a) for a in axes]
    blocks = blocks.reshape(*shape, *blocks.shape[1:])
    blocks = blocks.transpose(*order, *range(len(axes), blocks.ndim))
    blocks = blocks.reshape(-1, *blocks.shape[len(axes) :])
    for k in order:
        blocks = lax.psum_scatter(blocks, axes[k], scatter_dimension=0, tiled=True)
    return blocks[0]


def in_blocks(x, dim, peers):
    before, after = (x.shape[:dim], x.shape[dim + 1 :])
    return jnp.moveaxis(x.reshape(*before, peers, -1, *after), dim, 0)


def sum_by_axis(x, axes, order, dim):
    peers = lax.axis_size(axes)
    return reduced_to_own(in_blocks(x, dim, peers), axes, order)


def by_axis(x, axes):
    for axis in axes:
        x = lax.psum(x, axis)
    return x


def contract(left, right):
    return lax.dot_general(
        left, right, (((1,), (1,)), ((), ())), preferred_element_type=jnp.float32
    )


def contract_rows(left, right):
    return lax.dot_general(
        left, right, (((0,), (0,)), ((), ())), preferred_element_type=jnp.float32
    )


def forward(inputs, core_bf, head_bf):
    width = inputs.shape[-1]
    pre_one = contract(inputs, core_bf[:, :width])
    first_act = jax.nn.relu(pre_one)
    first_bf = first_act.astype(jnp.bfloat16)
    pre_two = contract(first_bf, core_bf[:, width:])
    second_act = jax.nn.relu(pre_two) + first_act
    second_bf = second_act.astype(jnp.bfloat16)
    network_outputs = contract(second_bf, head_bf)
    return (network_outputs, pre_one, first_bf, pre_two, second_bf)


def importance_trace_gradients(
    network_outputs, bootstrap_value, actions, done, rewards, behaviour, scale_factor
):
    action_count = network_outputs.shape[-1] - 1
    logits = network_outputs[..., :action_count]
    values = network_outputs[..., action_count]
    totals = jnp.sum(jnp.exp(logits), -1)
    logp = logits - jnp.log(totals)[..., None]
    probs = jnp.exp(logp)
    chosen = (actions[..., None] == jnp.arange(action_count, dtype=jnp.int32)).astype(jnp.float32)
    logp_act = jnp.sum(logp * chosen, -1)
    ratio = jnp.minimum(1.0, jnp.exp(logp_act - behaviour))
    discount = gamma_rate * (1.0 - done.astype(jnp.float32))
    next_values = jnp.concatenate([values[:, 1:], bootstrap_value[:, None]], 1)
    deltas = ratio * (rewards + discount * next_values - values)

    def backstep(carry, item):
        delta, factor = item
        carry = delta + factor * carry
        return (carry, carry)

    start = jnp.zeros((values.shape[0],), jnp.float32)
    final_carry, corrections = lax.scan(
        backstep, start, (deltas.T, (discount * ratio).T), reverse=True
    )
    targets = values + corrections.T
    next_targets = jnp.concatenate([targets[:, 1:], bootstrap_value[:, None]], 1)
    advantage = ratio * (rewards + discount * next_targets - values)
    entropy = -jnp.sum(probs * logp, -1)
    grad_logits = scale_factor * (
        -advantage[..., None] * (chosen - probs)
        + entropy_cost * probs * (logp + entropy[..., None])
    )
    grad_value = scale_factor * (-baseline_cost * (targets - values))
    return jnp.concatenate([grad_logits, grad_value[..., None]], -1)


def adam_step(master, moment, second, grad, rate):
    moment = beta_first * moment + (1.0 - beta_first) * grad
    second = beta_second * second + (1.0 - beta_second) * grad * grad
    master = master - rate * moment / (jnp.sqrt(second) + adam_eps)
    return (master, moment, second)


def per_device(
    learn_obs,
    own_obs,
    opp_obs,
    opponent,
    actions,
    done,
    rewards,
    behaviour,
    core_master,
    core_mom,
    core_vel,
    head_master,
    head_mom,
    head_vel,
    rates,
):
    environment_total, rollout_length, width = (
        learn_obs.shape[1],
        learn_obs.shape[2],
        learn_obs.shape[3],
    )
    action_count = head_master.shape[1] - 1
    agent_count = lax.axis_size("agent")
    slots = min(environment_total, BLOCK // agent_count)
    scale_factor = 1.0 / rollout_length
    core_bf = gather_axes(core_master.astype(jnp.bfloat16), DP, (0, 1), 1)[0]
    head_bf = head_master[0].astype(jnp.bfloat16)
    own_out = forward(own_obs[0], core_bf, head_bf)[0]
    ids = opponent[0, :, 0]
    earlier = (ids[None, :] == ids[:, None]) & jnp.tril(jnp.ones((ids.shape[0],) * 2, bool), -1)
    ranks = jnp.sum(earlier.astype(jnp.int32), 1)
    position = ids * slots + ranks
    placing = (
        position[None, :] == jnp.arange(agent_count * slots, dtype=jnp.int32)[:, None]
    ).astype(jnp.bfloat16)
    outgoing = jnp.dot(placing, opp_obs[0], preferred_element_type=jnp.float32).astype(jnp.bfloat16)
    outgoing = outgoing.reshape(agent_count, slots, width)
    incoming = lax.all_to_all(outgoing, "agent", split_axis=0, concat_axis=0, tiled=True)
    count = incoming.shape[1]
    played = forward(incoming.reshape(agent_count * count, width), core_bf, head_bf)[0][
        :, :action_count
    ]
    played = played.astype(jnp.bfloat16).reshape(agent_count, count, action_count)
    returned = lax.all_to_all(played, "agent", split_axis=0, concat_axis=0, tiled=True)
    opp_logits = returned.reshape(agent_count * slots, action_count)[position]
    rows = learn_obs[0].reshape(environment_total * rollout_length, width)
    network_outputs, pre_one, first_bf, pre_two, second_bf = forward(rows, core_bf, head_bf)
    output_gradient = importance_trace_gradients(
        network_outputs.reshape(environment_total, rollout_length, action_count + 1),
        own_out[:, action_count],
        actions[0],
        done[0],
        rewards[0],
        behaviour[0],
        scale_factor,
    )
    grad_bf = output_gradient.reshape(environment_total * rollout_length, action_count + 1).astype(
        jnp.bfloat16
    )
    head_grad = contract_rows(grad_bf, second_bf)
    grad_second = jnp.dot(grad_bf, head_bf, preferred_element_type=jnp.float32)
    grad_pre_two = jnp.where(pre_two > 0, grad_second, 0.0).astype(jnp.bfloat16)
    grad_first = grad_second + jnp.dot(
        grad_pre_two, core_bf[:, width:], preferred_element_type=jnp.float32
    )
    grad_pre_one = jnp.where(pre_one > 0, grad_first, 0.0).astype(jnp.bfloat16)
    core_grad = sum_by_axis(
        jnp.concatenate(
            [contract_rows(grad_pre_one, rows), contract_rows(grad_pre_two, first_bf)], 1
        ).astype(jnp.bfloat16),
        DP,
        (1, 0),
        0,
    ).astype(jnp.float32)
    head_total = by_axis(head_grad, DP)
    rate = rates[0]
    new_core, new_core_mom, new_core_vel = adam_step(
        core_master[0], core_mom[0], core_vel[0], core_grad, rate
    )
    new_head, new_head_mom, new_head_vel = adam_step(
        head_master[0], head_mom[0], head_vel[0], head_total, rate
    )
    return (
        own_out[:, :action_count][None],
        opp_logits[None],
        new_core[None],
        new_core_mom[None],
        new_core_vel[None],
        new_head[None],
        new_head_mom[None],
        new_head_vel[None],
    )


def solution(mesh):
    torus = Mesh(mesh.devices.reshape(mesh.shape["agent"], 16, 2), ("agent", "dp_0", "dp_1"))
    return jax.shard_map(
        per_device,
        mesh=torus,
        in_specs=(
            P("agent", DP, None, None),
            P("agent", DP, None),
            P("agent", DP, None),
            P("agent", DP, None),
            P("agent", DP, None),
            P("agent", DP, None),
            P("agent", DP, None),
            P("agent", DP, None),
            P("agent", DP, None),
            P("agent", DP, None),
            P("agent", DP, None),
            P("agent", None, None),
            P("agent", None, None),
            P("agent", None, None),
            P("agent"),
        ),
        out_specs=(
            P("agent", DP, None),
            P("agent", DP, None),
            P("agent", DP, None),
            P("agent", DP, None),
            P("agent", DP, None),
            P("agent", None, None),
            P("agent", None, None),
            P("agent", None, None),
        ),
        check_vma=False,
    )
```

profile of v0, /device:TPU:1, one launch (start us, length us, event | category | flops | bytes accessed | tf_op | source)
XLA Modules:
  0.0 268.0 jit_solution(14837776084978435782)
XLA Ops:
  8.3 37.6 %all-gather = bf16[16,8,3712]{2,1,0:T(8,128)(2,1)} all-gather(bf16[1,8,3712]{2,1,0:T(8,128)(2,1)S(1)} %convert_element_type.71), channel_id=2, replica_groups=mesh['agent'=16,'dp_0'=16,'dp_1'=2] {'dp_0'}, dimensions={0}, use_global_device_ids=true | all-gather | bytes 1009664 | tf_op jit(solution)/shard_map/all_gather | solution.py:28
  48.1 22.9 %all-gather.4.cloned.1.call-done = bf16[32,8,3712]{2,1,0:T(8,128)(2,1)} async-done(((bf16[16,8,3712]{2,1,0:T(8,128)(2,1)}), bf16[32,8,3712]{2,1,0:T(8,128)(2,1)}) %all-gather.4.cloned.1.call-update) | async-done | bytes 1900560 | tf_op jit(solution)/shard_map/all_gather | solution.py:28
  71.0 1.7 copy.180
  75.3 1.8 fusion.26
  77.1 2.6 fusion.4
  80.5 2.0 add_convert_fusion
  84.2 2.3 fusion.33
  91.6 40.4 %while.17 = (s32[]{:T(128)}, f32[32]{0:T(128)}, f32[16,32]{1,0:T(8,128)}, f32[16,32]{1,0:T(8,128)}, f32[16,32]{1,0:T(8,128)}, /*index=5*/s32[]{:T(128)}, s32[]{:T(128)}, s32[]{:T(128)}) while((s32[]{:T(128)}, f32[32]{0:T(128)}, f32[16,32]{1,0:T(8,128)}, f32[16,32]{1,0:T(8,128)}, f32[16,32]{1,0:T(8,128)}, /*index=5*/s32[]{:T(128)}, ...), condition=%wide.region_4.5_spmd.clone, body=%wide.region_3.4_spmd.clone.sunk | while | flops 100 | bytes 891 | solution.py:111
  140.2 1.9 fusion.31
  142.1 1.6 copy.189
  144.8 2.1 convolution_convert_fusion.2
  147.0 1.9 fusion.14
  148.9 1.8 copy.193
  150.7 2.1 convolution_convert_fusion
  155.2 2.2 fusion.3
  157.4 5.6 %all-to-all-start = ((bf16[16,8,3456]{2,1,0:T(8,128)(2,1)}), bf16[16,8,3456]{2,1,0:T(8,128)(2,1)}, u32[]{:S(2)}, u32[]{:S(2)}) async-start(bf16[16,8,3456]{2,1,0:T(8,128)(2,1)} %fusion.3), calls=%async_computation | async-start | bytes 1769472 | tf_op jit(solution)/shard_map/all_to_all | solution.py:171
  163.0 12.6 %reduce-scatter.5.cloned.1.call-done = bf16[16,8,3712]{2,1,0:T(8,128)(2,1)} async-done(((bf16[32,8,3712]{2,1,0:T(8,128)(2,1)}), bf16[16,8,3712]{2,1,0:T(8,128)(2,1)}) %reduce-scatter.5.cloned.1.call-update) | async-done | bytes 950288 | tf_op jit(solution)/shard_map/reduce_scatter | solution.py:45
  176.9 3.1 %fusion.15 = f32[128,256]{1,0:T(8,128)} fusion(bf16[256,3712]{1,0:T(8,128)(2,1)} %bitcast.156, bf16[16,8,3456]{2,1,0:T(8,128)(2,1)} %all-to-all-done), kind=kOutput, calls=%fused_computation.22 | convolution fusion | flops 226525184 | bytes 2785280 | tf_op jit(solution)/shard_map/dot_general | solution.py:66
  180.0 2.0 fusion.20
  183.4 5.7 %all-to-all-start.1 = ((bf16[16,8,18]{2,1,0:T(8,128)(2,1)}), bf16[16,8,18]{2,1,0:T(8,128)(2,1)}, u32[]{:S(2)}, u32[]{:S(2)}) async-start(bf16[16,8,18]{2,1,0:T(8,128)(2,1)} %bitcast.164), calls=%async_computation.1 | async-start | bytes 65536 | tf_op jit(solution)/shard_map/all_to_all | solution.py:177
  189.2 1.7 fusion.56
  190.9 45.8 %psum.14 = f32[19,256]{1,0:T(8,128)} all-reduce(f32[19,256]{1,0:T(8,128)} %fusion.56), channel_id=1, replica_groups=mesh['agent'=16,'dp_0'=16,'dp_1'=2] {'dp_0'}, use_global_device_ids=true, to_apply=%region_8.9 | all-reduce | flops 4864 | bytes 38912 | tf_op jit(solution)/shard_map/psum | solution.py:61
  236.7 17.5 %psum.15 = f32[19,256]{1,0:T(8,128)} all-reduce(f32[19,256]{1,0:T(8,128)} %psum.14), channel_id=1, replica_groups=mesh['agent'=16,'dp_0'=16,'dp_1'=2] {'dp_1'}, use_global_device_ids=true, to_apply=%region_9.10 | all-reduce | flops 4864 | bytes 38912 | tf_op jit(solution)/shard_map/psum | solution.py:61
  259.7 1.8 divide_subtract_fusion
  (104 shorter events, 73.0 us)
Async XLA Ops:
  7.2 69.9 %copy-start = (bf16[1,32,16,3456]{3,2,1,0:T(8,128)(2,1)S(1)}, bf16[1,32,16,3456]{3,2,1,0:T(8,128)(2,1)}, u32[]{:S(2)}) copy-start(bf16[1,32,16,3456]{3,2,1,0:T(8,128)(2,1)} %param.17) | copy-start | bytes 10616836
  7.2 63.8 %all-gather.4.cloned.1.call-start = ((), (), s32[]{:S(2)}) async-start(), calls=%async_computation.5 | async-start | bytes 2850816 | tf_op jit(solution)/shard_map/all_gather | solution.py:28
  46.0 129.6 %reduce-scatter.5.cloned.1.call-start = ((), (), s32[]{:S(2)}) async-start(), calls=%async_computation.4 | async-start | bytes 2850816 | tf_op jit(solution)/shard_map/reduce_scatter | solution.py:45
  46.8 37.5 %copy-start.7 = (s32[32,16]{1,0:T(8,128)}, s32[32,16]{1,0:T(8,128)S(1)}, u32[]{:S(2)}) copy-start(s32[32,16]{1,0:T(8,128)S(1)} %copy.182) | copy-start | bytes 6148
  71.0 3.0 %copy-start.12 = (bf16[1,32,3456]{2,1,0:T(8,128)(2,1)S(1)}, bf16[1,32,3456]{2,1,0:T(8,128)(2,1)}, u32[]{:S(2)}) copy-start(bf16[1,32,3456]{2,1,0:T(8,128)(2,1)} %param.18) | copy-start | bytes 663556
  72.7 1.3 copy-start.4
  77.1 6.1 %copy-start.8 = (bf16[1,19,256]{2,0,1:T(2,128)(2,1)S(1)}, bf16[1,19,256]{2,0,1:T(2,128)(2,1)}, u32[]{:S(2)}) copy-start(bf16[1,19,256]{2,0,1:T(2,128)(2,1)} %convert_element_type.81) | copy-start | bytes 29188
  79.7 0.8 copy-start.1
  82.5 0.7 copy-start.5
  143.7 3.3 %copy-start.2 = (f32[512,256]{1,0:T(8,128)S(1)}, f32[512,256]{1,0:T(8,128)}, u32[]{:S(2)}) copy-start(f32[512,256]{1,0:T(8,128)} %copy-done.1) | copy-start | bytes 1572868
  143.7 3.3 %copy-start.3 = (f32[512,256]{1,0:T(8,128)S(1)}, f32[512,256]{1,0:T(8,128)}, u32[]{:S(2)}) copy-start(f32[512,256]{1,0:T(8,128)} %get-tuple-element.223) | copy-start | bytes 1572868
  150.7 2.1 copy-start.6
  154.3 0.7 copy-start.11
  157.4 19.5 %all-to-all-start = ((bf16[16,8,3456]{2,1,0:T(8,128)(2,1)}), bf16[16,8,3456]{2,1,0:T(8,128)(2,1)}, u32[]{:S(2)}, u32[]{:S(2)}) async-start(bf16[16,8,3456]{2,1,0:T(8,128)(2,1)} %fusion.3), calls=%async_computation | async-start | bytes 1769472 | tf_op jit(solution)/shard_map/all_to_all | solution.py:171
  163.0 96.7 %reduce-scatter.7.cloned.1.call-start = ((), (), s32[]{:S(2)}) async-start(), calls=%async_computation.6 | async-start | bytes 1009664
  175.6 13.5 %copy-start.10 = (bf16[512,1]{0,1:T(2,128)(2,1)S(1)}, bf16[512,1]{0,1:T(2,128)(2,1)}, u32[]{:S(2)}) copy-start(bf16[512,1]{0,1:T(2,128)(2,1)} %concatenate.38) | copy-start | bytes 3076
  176.9 78.1 %copy-start.9 = (f32[32,19]{0,1:T(8,128)S(1)}, f32[32,19]{0,1:T(8,128)}, u32[]{:S(2)}) copy-start(f32[32,19]{0,1:T(8,128)} %fusion.26) | copy-start | bytes 7300
  183.4 74.1 %all-to-all-start.1 = ((bf16[16,8,18]{2,1,0:T(8,128)(2,1)}), bf16[16,8,18]{2,1,0:T(8,128)(2,1)}, u32[]{:S(2)}, u32[]{:S(2)}) async-start(bf16[16,8,18]{2,1,0:T(8,128)(2,1)} %bitcast.164), calls=%async_computation.1 | async-start | bytes 65536 | tf_op jit(solution)/shard_map/all_to_all | solution.py:177
Sparse Core Ops, SparseCore 0:
  46.1 24.8 all-gather.3
  154.5 21.0 reduce-scatter.4
  178.7 60.5 reduce-scatter.6
where the time goes:
time: 271 us; the launch traced here: 268 us
  blocking collectives  101 us (37%)
  local copies, waits for them, and re-layouts  46.2 us (17%)
  waiting for transfers between devices  35.5 us (13%)
  other arithmetic  35.2 us (13%)
  matrix products  24.1 us (9%)
  between operations  14.6 us (5%)
  starting transfers between devices  11.4 us (4%)
    psum x2, blocking collectives, by_axis(): x = lax.psum(x, axis)  63.3 us
    all_gather x1, blocking collectives, stacked_from(): blocks = lax.all_gather(blocks, axes[k], axis=0, tiled=True)  37.6 us
    all_gather x1, waiting for transfers between devices, stacked_from(): blocks = lax.all_gather(blocks, axes[k], axis=0, tiled=True)  22.9 us
    dynamic_update_slice x16, local copies, waits for them, and re-layouts, importance_trace_gradients(): lax.scan(backstep, start, (deltas.T, (discount * ratio).T), reverse=True)  20.6 us
    add x16, other arithmetic, backstep(): carry = delta + factor * carry  19.8 us
    dot_general x7, matrix products, contract(): lax.dot_general(left, right, (((1,), (1,)), ((), ())), preferred_element_...  13 us
    reduce_scatter x1, waiting for transfers between devices, reduced_to_own(): blocks = lax.psum_scatter(blocks, axes[k], scatter_dimension=0, tiled=True)  12.6 us
    unnamed x32, local copies, waits for them, and re-layouts  7.75 us
  transfers between devices with their start and end apart: 5, of which 2 were waited for; matrix products, arithmetic and copies ran while one was open for 7% of the time, Pallas kernels for 0%

commit v1 on v0

v1 whole, which is shorter than its diff:
```python
import functools

import jax
import jax.numpy as jnp
from jax import lax
from jax.experimental import pallas as pl
from jax.experimental.pallas import tpu as pltpu
from jax.sharding import PartitionSpec as P

MESH = pl.DeviceIdType.MESH
F32 = jnp.float32
BF16 = jnp.bfloat16
SLOTS = 8
PAD = 128
CHUNKS = 4

gamma_rate = 0.99
baseline_cost = 0.5
entropy_cost = 0.05
beta_first = 0.9
beta_second = 0.99
adam_eps = 1e-08


def dot(left, right, dims=((1,), (0,)), precision=None):
    return lax.dot_general(left, right, (dims, ((), ())), precision=precision, preferred_element_type=F32)


def bounds(total, parts, unit=128):
    units = -(-total // unit)
    return [min(total, unit * (units * i // parts)) for i in range(parts + 1)]


def column(row_vector, sublanes):
    return jnp.broadcast_to(row_vector, (sublanes, row_vector.shape[1]))


def trace_gradient(out, boot, actions, done, rewards, behaviour, actions_total, steps):
    rows, frames = out.shape
    scale = 1.0 / steps
    row = lax.broadcasted_iota(jnp.int32, (rows, frames), 0)
    time = lax.broadcasted_iota(jnp.int32, (8, frames), 1) % steps
    is_logit = row < actions_total
    values = column(out[actions_total : actions_total + 1, :], 8)
    total = jnp.sum(jnp.where(is_logit, jnp.exp(out), 0.0), 0, keepdims=True)
    logp = out - jnp.log(total)
    probs = jnp.where(is_logit, jnp.exp(logp), 0.0)
    chosen = (row.astype(F32) == actions).astype(F32)
    logp_act = jnp.sum(jnp.where(is_logit, logp, 0.0) * chosen, 0, keepdims=True)
    entropy = -jnp.sum(probs * jnp.where(is_logit, logp, 0.0), 0, keepdims=True)
    ratio = column(jnp.minimum(1.0, jnp.exp(logp_act - behaviour)), 8)
    discount = column(gamma_rate * (1.0 - done), 8)
    rewards, boot = column(rewards, 8), column(boot, 8)
    last = time == steps - 1

    def later(x, by):
        return pltpu.roll(x, frames - by, 1)

    next_values = jnp.where(last, boot, later(values, 1))
    corr = ratio * (rewards + discount * next_values - values)
    factor = discount * ratio
    by = 1
    while by < steps:
        inside = time < steps - by
        corr, factor = (
            corr + factor * jnp.where(inside, later(corr, by), 0.0),
            factor * jnp.where(inside, later(factor, by), 0.0),
        )
        by *= 2
    targets = values + corr
    next_targets = jnp.where(last, boot, later(targets, 1))
    advantage = ratio * (rewards + discount * next_targets - values)
    grad_logits = scale * (
        -advantage[:1] * (chosen - probs) + entropy_cost * probs * (logp + entropy)
    )
    grad_value = scale * (-baseline_cost * (targets - values))[:1]
    return jnp.where(is_logit, grad_logits, jnp.where(row == actions_total, grad_value, 0.0))


def step_kernel(
    sizes,
    learn_hbm, own_hbm, opp_hbm, opponent_hbm, actions_hbm, done_hbm, rewards_hbm, behaviour_hbm, core_hbm, head_hbm,
    grad_out, head_out, own_out, opp_out,
    x, own, opp, opponent, actions, done, rewards, behaviour, core, head,
    shards, weights, pre, mine, for_sibling, from_sibling, sums_out, sums_in, frames_out, frames_in,
    played_out, played_in, heads, head_part, head_from, head_all, head_final,
    load_sem, gather_send, gather_recv, pair_send, pair_recv, own_send, own_recv,
    frame_send, frame_recv, played_send, played_recv, reduce_send, reduce_recv,
    half_send, half_recv, hring_send, hring_recv, hpair_send, hpair_recv, hlast_send, hlast_recv,
):
    (agents, chips, shard, envs, steps, feat, units, head_rows, agent_y) = sizes
    frames = envs * steps
    width = feat + units
    acts = head_rows - 1
    edges = bounds(width, CHUNKS)
    far = chips // 2
    half = CHUNKS // 2
    agent, dp = lax.axis_index("agent"), lax.axis_index("dp")
    chip, side = dp // 2, dp % 2
    other = 1 - side
    agent_x = agents // agent_y
    ax, ay = agent // agent_y, agent % agent_y

    def chip_at(offset):
        return lax.rem(chip + (offset + 2 * chips), chips)

    sibling = (agent, 2 * chip + other)
    ring = [(agent, 2 * chip_at(1) + side), (agent, 2 * chip_at(-1) + side)]
    sign = [1, -1]
    shifts = [(i, j) for i in range(agent_x) for j in range(agent_y) if (i, j) != (0, 0)]
    to_agent = [lax.rem(ax + i, agent_x) * agent_y + lax.rem(ay + j, agent_y) for i, j in shifts]
    from_agent = [lax.rem(ax + agent_x - i, agent_x) * agent_y + lax.rem(ay + agent_y - j, agent_y) for i, j in shifts]

    barrier = pltpu.get_barrier_semaphore()
    peers = [sibling, *ring, *[(a, dp) for a in to_agent]]
    for peer in peers:
        pl.semaphore_signal(barrier, inc=1, device_id=peer, device_id_type=MESH)

    loads = [
        pltpu.make_async_copy(src, dst, load_sem.at[i])
        for i, (src, dst) in enumerate((
            (core_hbm.at[0], core), (head_hbm.at[0], head), (opponent_hbm.at[0], opponent), (opp_hbm.at[0], opp),
            (learn_hbm.at[0], x), (own_hbm.at[0], own), (actions_hbm.at[0], actions), (done_hbm.at[0], done),
            (rewards_hbm.at[0], rewards), (behaviour_hbm.at[0], behaviour),
        ))
    ]
    for load in loads:
        load.start()

    def cols(f):
        return pl.ds(edges[f], edges[f + 1] - edges[f])

    def remote(src, dst, send, recv, to):
        return pltpu.make_async_remote_copy(
            src_ref=src, dst_ref=dst, send_sem=send, recv_sem=recv, device_id=to, device_id_type=MESH
        )

    def gather_has(way, s, f):
        return s < far - 1 or (f < half) == (way == 0)

    def gather(way, s, f):
        block = shards.at[chip_at(-sign[way] * s), side, :, cols(f)]
        return remote(block, block, gather_send.at[way, s, f], gather_recv.at[way, s, f], ring[way])

    def gathered(way, s, f):
        block = shards.at[chip_at(-sign[way] * (s + 1)), side, :, cols(f)]
        return remote(block, block, gather_send.at[way, s, f], gather_recv.at[way, s, f], ring[way])

    def pair(way, s, f, which):
        block = shards.at[chip_at(-sign[way] * (s + 1)), which, :, cols(f)]
        return remote(block, block, pair_send.at[way, s, f], pair_recv.at[way, s, f], sibling)

    def own_pair(which):
        block = shards.at[chip, which]
        return remote(block, block, own_send, own_recv, sibling)

    loads[0].wait()
    shards[chip, side] = core[...].astype(BF16)
    pl.semaphore_wait(barrier, len(peers))
    for f in range(CHUNKS):
        for way in (0, 1):
            if gather_has(way, 0, f):
                gather(way, 0, f).start()
    own_pair(side).start()

    for load in loads[1:4]:
        load.wait()
    ids = opponent[...]
    agent_lane = lax.broadcasted_iota(jnp.int32, (envs, PAD), 1)
    member = (ids == agent_lane).astype(F32)
    before = (
        lax.broadcasted_iota(jnp.int32, (envs, envs), 1) < lax.broadcasted_iota(jnp.int32, (envs, envs), 0)
    ).astype(F32)
    ranks = jnp.sum(dot(before.astype(BF16), member.astype(BF16)) * member, 1, keepdims=True)
    position = ids * SLOTS + ranks.astype(jnp.int32)
    lane = lax.broadcasted_iota(jnp.int32, (envs, agents * SLOTS), 1)
    placing = (position == lane).astype(F32)
    placed = placing.T.astype(BF16)
    placing = placing.astype(BF16)
    outgoing = dot(placed, opp[...]).reshape(agents, SLOTS, feat).astype(BF16)
    frames_out[...] = outgoing
    frames_in[agent] = frames_out[agent]

    def send_frames(i):
        return remote(
            frames_out.at[to_agent[i]], frames_in.at[agent], frame_send.at[i], frame_recv.at[i], (to_agent[i], dp)
        )

    def frames_come(i):
        return remote(
            frames_out.at[to_agent[i]], frames_in.at[from_agent[i]], frame_send.at[i], frame_recv.at[i], (to_agent[i], dp)
        )

    for i in range(len(shifts)):
        send_frames(i).start()

    heads[...] = jnp.zeros_like(heads)
    heads[0:head_rows, :] = head[...]
    head_bf = heads[...].astype(BF16)
    head_turned = heads[...].T.astype(BF16)
    small = head_bf[:32]

    for load in loads[6:]:
        load.wait()
    stacked = jnp.concatenate(
        [actions[...].astype(F32), done[...].astype(F32), rewards[...], behaviour[...]], 0
    )
    spread = (
        lax.broadcasted_iota(jnp.int32, (steps, frames), 1) % steps
        == lax.broadcasted_iota(jnp.int32, (steps, frames), 0)
    ).astype(F32)
    env_row = lax.broadcasted_iota(jnp.int32, (envs, frames), 0)
    env_lane = lax.broadcasted_iota(jnp.int32, (envs, frames), 1)
    same_env = env_lane // steps == env_row
    spread = dot(stacked, spread, precision=lax.Precision.HIGHEST).reshape(4, envs, frames)
    flat = jnp.sum(jnp.where(same_env[None], spread, 0.0), 1)

    loads[4].wait()
    loads[5].wait()

    def repack(at, f):
        pair_of = [shards[at, k, :, cols(f)].astype(F32) for k in (0, 1)]
        weights[at, :, cols(f)] = jnp.concatenate(pair_of, 0).astype(BF16)

    def weight_cols(lo, hi):
        return weights[:, :, lo:hi].reshape(units, hi - lo)

    def frame_cols(lo, hi):
        return x[:, :, lo:hi].reshape(frames, hi - lo)

    def layer_one(f, total, own_total):
        lo, hi = edges[f], min(edges[f + 1], feat)
        if lo >= hi:
            return total, own_total
        part = weight_cols(lo, hi)
        one = dot(part, frame_cols(lo, hi), ((1,), (1,)))
        two = dot(own[:, lo:hi], part, ((1,), (1,)))
        return (one, two) if total is None else (total + one, own_total + two)

    total, own_total = None, None
    for s in range(far):
        for f in range(CHUNKS):
            for way in (0, 1):
                if gather_has(way, s, f):
                    gathered(way, s, f).wait_recv()
                    if s + 1 < far and gather_has(way, s + 1, f):
                        gather(way, s + 1, f).start()
                    pair(way, s, f, side).start()
            if s == 0 and f == 0:
                own_pair(other).wait_recv()
            for way in (0, 1):
                if s == 0:
                    if way == 0:
                        repack(chip, f)
                else:
                    pair(way, s - 1, f, other).wait_recv()
                    repack(chip_at(-sign[way] * s), f)
            if s == far - 1 and f > 0:
                way = 0 if f - 1 < half else 1
                pair(way, s, f - 1, other).wait_recv()
                repack(chip_at(-sign[way] * (s + 1)), f - 1)
                total, own_total = layer_one(f - 1, total, own_total)
    way = 0 if CHUNKS - 1 < half else 1
    pair(way, far - 1, CHUNKS - 1, other).wait_recv()
    repack(chip_at(-sign[way] * far), CHUNKS - 1)
    total, own_total = layer_one(CHUNKS - 1, total, own_total)

    second = weight_cols(feat, width)
    second_turned = second.astype(F32).T.astype(BF16)

    def narrow(first):
        act = jnp.maximum(first, 0.0)
        late = dot(act.astype(BF16), second, ((1,), (1,)))
        act = jnp.maximum(late, 0.0) + act
        return dot(act.astype(BF16), head_bf, ((1,), (1,)))

    own_net = narrow(own_total)
    own_out[...] = own_net
    boot = jnp.sum(jnp.where(env_lane == env_row * steps + steps - 1, own_net[:, acts : acts + 1], 0.0), 0, keepdims=True)

    act_one = jnp.maximum(total, 0.0)
    one_bf = act_one.astype(BF16)
    pre_two = dot(second, one_bf)
    two_bf = (jnp.maximum(pre_two, 0.0) + act_one).astype(BF16)
    net = dot(small, two_bf)
    out_grad = trace_gradient(net, boot, flat[0:1], flat[1:2], flat[2:3], flat[3:4], acts, steps).astype(BF16)

    head_grad = dot(out_grad, two_bf, ((1,), (1,)))
    half_units = units // 2
    for k in (0, 1):
        head_part[k] = head_grad[0:24, k * half_units : (k + 1) * half_units]
    hpair = remote(head_part.at[other], head_from, hpair_send, hpair_recv, sibling)
    hpair.start()

    g_two = dot(head_turned[:, :32], out_grad)
    gp_two = jnp.where(pre_two > 0, g_two, 0.0).astype(BF16)
    g_one = g_two + dot(second_turned, gp_two)
    gp_one = jnp.where(total > 0, g_one, 0.0).astype(BF16)

    hpair.wait_recv()
    head_all[chip] = head_part[side] + head_from[...]

    def head_ring(way, s):
        block = head_all.at[chip_at(-sign[way] * s)]
        return remote(block, block, hring_send.at[way, s], hring_recv.at[way, s], ring[way])

    def head_come(way, s):
        block = head_all.at[chip_at(-sign[way] * (s + 1))]
        return remote(block, block, hring_send.at[way, s], hring_recv.at[way, s], ring[way])

    def head_has(way, s):
        return s < far - 1 or way == 0

    for way in (0, 1):
        if head_has(way, 0):
            head_ring(way, 0).start()

    def swap(f):
        return remote(
            for_sibling.at[:, :, cols(f)], from_sibling.at[:, :, cols(f)], half_send.at[f], half_recv.at[f], sibling
        )

    first_side = side == 0
    for f in range(CHUNKS):
        lo, hi = edges[f], edges[f + 1]
        parts = []
        if lo < feat:
            parts.append(dot(gp_one, frame_cols(lo, min(hi, feat))))
        if hi > feat:
            parts.append(dot(gp_two, one_bf, ((1,), (1,))))
        grad = parts[0] if len(parts) == 1 else jnp.concatenate(parts, 1)
        grad = grad.reshape(chips, 2, shard, hi - lo)
        for_sibling[:, :, lo:hi] = jnp.where(first_side, grad[:, 1], grad[:, 0]).astype(BF16)
        swap(f).start()
        mine[:, :, lo:hi] = jnp.where(first_side, grad[:, 0], grad[:, 1])

    def reduce_has(way, s, f):
        return s > 0 or (f < half) == (way == 0)

    def reduce_to(way, s, f):
        return remote(
            sums_out.at[way, s, :, cols(f)], sums_in.at[way, s, :, cols(f)],
            reduce_send.at[way, s, f], reduce_recv.at[way, s, f], ring[way],
        )

    def reduce_step(way, s, f):
        term = mine[chip_at(sign[way] * (far - s)), :, cols(f)]
        if s > 0 and reduce_has(way, s - 1, f):
            reduce_to(way, s - 1, f).wait_recv()
            term = term + sums_in[way, s - 1, :, cols(f)].astype(F32)
        sums_out[way, s, :, cols(f)] = term.astype(BF16)
        reduce_to(way, s, f).start()

    for f in range(CHUNKS):
        swap(f).wait_recv()
        lo, hi = edges[f], edges[f + 1]
        mine[:, :, lo:hi] = mine[:, :, lo:hi] + from_sibling[:, :, lo:hi].astype(F32)
        for way in (0, 1):
            if reduce_has(way, 0, f):
                reduce_step(way, 0, f)

    for s in range(1, far):
        for way in (0, 1):
            if head_has(way, s - 1):
                head_come(way, s - 1).wait_recv()
                if head_has(way, s):
                    head_ring(way, s).start()
        for f in range(CHUNKS):
            for way in (0, 1):
                reduce_step(way, s, f)
        if s == min(2, far - 1):
            for i in range(len(shifts)):
                frames_come(i).wait_recv()
            came = frames_in[...].astype(F32).reshape(agents * SLOTS, feat).astype(BF16)
            answers = narrow(dot(came, weight_cols(0, feat), ((1,), (1,))))
            played_out[...] = answers.reshape(agents, SLOTS, PAD).astype(BF16)
            played_in[agent] = played_out[agent]
            for i in range(len(shifts)):
                remote(
                    played_out.at[to_agent[i]], played_in.at[agent], played_send.at[i], played_recv.at[i], (to_agent[i], dp)
                ).start()

    for way in (0, 1):
        if head_has(way, far - 1):
            head_come(way, far - 1).wait_recv()
    head_final[side] = jnp.sum(head_all[...], 0)
    hlast = remote(head_final.at[side], head_final.at[side], hlast_send, hlast_recv, sibling)
    hlast.start()

    def played_come(i):
        return remote(
            played_out.at[to_agent[i]], played_in.at[from_agent[i]], played_send.at[i], played_recv.at[i], (to_agent[i], dp)
        )

    for i in range(len(shifts)):
        played_come(i).wait_recv()
    back = played_in[...].astype(F32).reshape(agents * SLOTS, PAD).astype(BF16)
    opp_out[...] = dot(placing, back).astype(BF16)

    for f in range(CHUNKS):
        total = mine[chip, :, cols(f)]
        for way in (0, 1):
            reduce_to(way, far - 1, f).wait_recv()
            total = total + sums_in[way, far - 1, :, cols(f)].astype(F32)
        grad_out[:, cols(f)] = total

    remote(head_final.at[other], head_final.at[other], hlast_send, hlast_recv, sibling).wait_recv()
    head_out[...] = head_final[...]

    for s in range(far):
        for f in range(CHUNKS):
            for way in (0, 1):
                if gather_has(way, s, f):
                    gather(way, s, f).wait_send()
                    pair(way, s, f, side).wait_send()
                if reduce_has(way, s, f):
                    reduce_to(way, s, f).wait_send()
        for way in (0, 1):
            if head_has(way, s):
                head_ring(way, s).wait_send()
    own_pair(side).wait_send()
    hpair.wait_send()
    hlast.wait_send()
    for f in range(CHUNKS):
        swap(f).wait_send()
    for i in range(len(shifts)):
        send_frames(i).wait_send()
        played_come(i).wait_send()


def adam_step(master, moment, second, grad, rate):
    moment = beta_first * moment + (1.0 - beta_first) * grad
    second = beta_second * second + (1.0 - beta_second) * grad * grad
    master = master - rate * moment / (jnp.sqrt(second) + adam_eps)
    return (master, moment, second)


def per_device(
    learn_obs, own_obs, opp_obs, opponent, actions, done, rewards, behaviour,
    core_master, core_mom, core_vel, head_master, head_mom, head_vel, rates,
):
    _, envs, steps, feat = learn_obs.shape
    _, shard, width = core_master.shape
    _, head_rows, units = head_master.shape
    agents, dp = lax.axis_size("agent"), lax.axis_size("dp")
    chips = dp // 2
    far = chips // 2
    agent_y = 4 if agents % 4 == 0 else agents
    sizes = (agents, chips, shard, envs, steps, feat, units, head_rows, agent_y)
    vmem, dma = pltpu.VMEM, pltpu.SemaphoreType.DMA
    shifts = agents - 1
    anywhere = pl.BlockSpec(memory_space=pl.ANY)
    in_vmem = pl.BlockSpec(memory_space=vmem)
    grad, head_grad, own_net, opp_net = pl.pallas_call(
        functools.partial(step_kernel, sizes),
        out_shape=(
            jax.ShapeDtypeStruct((shard, width), F32),
            jax.ShapeDtypeStruct((2, 24, units // 2), F32),
            jax.ShapeDtypeStruct((envs, PAD), F32),
            jax.ShapeDtypeStruct((envs, PAD), BF16),
        ),
        in_specs=[anywhere] * 10,
        out_specs=(in_vmem,) * 4,
        scratch_shapes=[
            vmem((envs, steps, feat), BF16),
            vmem((envs, feat), BF16),
            vmem((envs, feat), BF16),
            vmem((envs, 1), jnp.int32),
            vmem((envs, steps), jnp.int32),
            vmem((envs, steps), jnp.int32),
            vmem((envs, steps), F32),
            vmem((envs, steps), F32),
            vmem((shard, width), F32),
            vmem((head_rows, units), F32),
            vmem((chips, 2, shard, width), BF16),
            vmem((chips, 2 * shard, width), BF16),
            vmem((8, 128), F32),
            vmem((chips, shard, width), F32),
            vmem((chips, shard, width), BF16),
            vmem((chips, shard, width), BF16),
            vmem((2, far, shard, width), BF16),
            vmem((2, far, shard, width), BF16),
            vmem((agents, SLOTS, feat), BF16),
            vmem((agents, SLOTS, feat), BF16),
            vmem((agents, SLOTS, PAD), BF16),
            vmem((agents, SLOTS, PAD), BF16),
            vmem((PAD, units), F32),
            vmem((2, 24, units // 2), F32),
            vmem((24, units // 2), F32),
            vmem((chips, 24, units // 2), F32),
            vmem((2, 24, units // 2), F32),
            dma((10,)),
            dma((2, far, CHUNKS)),
            dma((2, far, CHUNKS)),
            dma((2, far, CHUNKS)),
            dma((2, far, CHUNKS)),
            dma,
            dma,
            dma((shifts,)),
            dma((shifts,)),
            dma((shifts,)),
            dma((shifts,)),
            dma((2, far, CHUNKS)),
            dma((2, far, CHUNKS)),
            dma((CHUNKS,)),
            dma((CHUNKS,)),
            dma((2, far)),
            dma((2, far)),
            dma,
            dma,
            dma,
            dma,
        ],
        compiler_params=pltpu.CompilerParams(
            collective_id=0, has_side_effects=True, vmem_limit_bytes=56 * 2**20
        ),
    )(learn_obs, own_obs, opp_obs, opponent, actions, done, rewards, behaviour, core_master, head_master)
    head_total = jnp.concatenate([head_grad[0, :head_rows], head_grad[1, :head_rows]], 1)
    rate = rates[0]
    new_core = adam_step(core_master[0], core_mom[0], core_vel[0], grad, rate)
    new_head = adam_step(head_master[0], head_mom[0], head_vel[0], head_total, rate)
    return (
        own_net[None, :, : head_rows - 1],
        opp_net[None, :, : head_rows - 1],
        *[a[None] for a in new_core],
        *[a[None] for a in new_head],
    )


def solution(mesh):
    rows, whole = P("agent", "dp"), P("agent")
    return jax.shard_map(
        per_device,
        mesh=mesh,
        in_specs=(rows,) * 11 + (whole,) * 4,
        out_specs=(rows,) * 5 + (whole,) * 3,
        check_vma=False,
    )
```

time: 271 us -> 96.3 us (0.36)
  blocking collectives: 101 us -> 0 us
  Pallas kernels: 0 us -> 78.9 us
  waiting for transfers between devices: 35.5 us -> 0 us
  other arithmetic: 35.2 us -> 1.74 us
  local copies, waits for them, and re-layouts: 46.2 us -> 13.7 us
  matrix products: 24.1 us -> 0 us
  between operations: 14.6 us -> 1.38 us
  starting transfers between devices: 11.4 us -> 0 us
    pallas_call x0 -> x1, Pallas kernels: none -> 78.9 us  [per_device(): pl.pallas_call(functools.partial(step_kernel, sizes), out_shape=(jax.Shap...]
    psum x2 -> x0, blocking collectives: 63.3 us -> none  [by_axis(): x = lax.psum(x, axis)]
    all_gather x1 -> x0, blocking collectives: 37.6 us -> none  [stacked_from(): blocks = lax.all_gather(blocks, axes[k], axis=0, tiled=True)]
    dot_general x13 -> x0, matrix products: 24.1 us -> none  [the longest x7 13 us: contract(): lax.dot_general(left, right, (((1,), (1,)), ((), ())), preferred_element_...]
    all_gather x1 -> x0, waiting for transfers between devices: 22.9 us -> none  [stacked_from(): blocks = lax.all_gather(blocks, axes[k], axis=0, tiled=True)]
    add x19 -> x0, other arithmetic: 21.1 us -> none  [the longest x16 19.8 us: backstep(): carry = delta + factor * carry]
    dynamic_update_slice x16 -> x0, local copies, waits for them, and re-layouts: 20.6 us -> none  [importance_trace_gradients(): lax.scan(backstep, start, (deltas.T, (discount * ratio).T), reverse=True)]
    reduce_scatter x1 -> x0, waiting for transfers between devices: 12.6 us -> none  [reduced_to_own(): blocks = lax.psum_scatter(blocks, axes[k], scatter_dimension=0, tiled=True)]
  transfers between devices with their start and end apart: 5 -> 0, of which waited for: 2 -> 0; matrix products, arithmetic and copies ran while one was open for 7% -> 0% of each run, Pallas kernels for 0% -> 0%
where the time goes in v1:
time: 96.3 us; the launch traced here: 95.7 us
  Pallas kernels  78.9 us (82%)
  local copies, waits for them, and re-layouts  13.7 us (14%)
  other arithmetic  1.74 us (2%)
  between operations  1.38 us (1%)
    pallas_call x1, Pallas kernels, per_device(): pl.pallas_call(functools.partial(step_kernel, sizes), out_shape=(jax.Shap...  78.9 us
    unnamed x23, local copies, waits for them, and re-layouts  11.5 us

profile of v1, /device:TPU:1, one launch (start us, length us, event | category | flops | bytes accessed | tf_op | source)
XLA Modules:
  0.0 95.7 jit_solution(750250578641644353)
XLA Ops:
  0.6 0.0 copy-start
  0.6 0.0 copy-start.3
  0.7 0.0 copy-start.1
  0.7 0.0 copy-start.2
  0.7 0.0 copy-start.4
  0.7 0.0 copy-start.5
  0.7 1.4 %copy.23.opponent_hbm = s32[1,32,1]{2,1,0:T(8,128)} copy(s32[1,32,1]{1,2,0:T(1,128)} %param.18) | data formatting | bytes 256 | tf_op args[3]
  2.1 1.4 %copy.24.actions_hbm = s32[1,32,16]{2,1,0:T(8,128)} copy(s32[1,32,16]{1,2,0:T(8,128)} %param.19) | data formatting | bytes 4096 | tf_op args[4]
  3.5 1.4 %copy.25.done_hbm = s32[1,32,16]{2,1,0:T(8,128)} copy(s32[1,32,16]{1,2,0:T(8,128)} %param.20) | data formatting | bytes 4096 | tf_op args[5]
  4.9 1.4 %copy.26.rewards_hbm = f32[1,32,16]{2,1,0:T(8,128)} copy(f32[1,32,16]{1,2,0:T(8,128)} %param.21) | data formatting | bytes 4096 | tf_op args[6]
  6.3 1.4 %copy.27.behaviour_hbm = f32[1,32,16]{2,1,0:T(8,128)} copy(f32[1,32,16]{1,2,0:T(8,128)} %param.22) | data formatting | bytes 4096 | tf_op args[7]
  7.6 1.3 %copy.28.head_hbm = f32[1,19,256]{2,1,0:T(8,128)} copy(f32[1,19,256]{2,0,1:T(1,128)} %param.26) | data formatting | bytes 38912 | tf_op args[11]
  9.0 78.9 %shard_map.206 = (f32[8,3712]{1,0:T(8,128)}, f32[2,24,128]{2,1,0:T(8,128)}, f32[32,128]{1,0:T(8,128)}, bf16[32,128]{1,0:T(8,128)(2,1)}) custom-call(bf16[1,32,16,3456]{3,2,1,0:T(8,128)(2,1)} %learn_hbm.1, bf16[1,32,3456]{2,1,0:T(8,128)(2,1)} %own_hbm.1, bf16[1,32,3456]{2,1,0:T(8,128)(2,1)} %opp_hbm.1, s32[1,32,1]{2,1,0:T(8,128)} %copy.23.opponent_hbm, ...), custom_call_target="tpu_custom_call" | custom-call | tf_op jit(solution)/shard_map/pallas_call | solution.py:454
  87.9 0.7 slice_bitcast_fusion
  88.6 0.7 copy.32
  89.3 0.7 slice_bitcast_fusion.1
  90.0 0.7 copy.33
  91.3 0.0 copy-done
  91.3 0.0 copy-done.1
  91.4 1.7 %fusion.3 = (f32[1,8,3712]{2,1,0:T(8,128)}, f32[1,8,3712]{2,1,0:T(8,128)}, f32[1,8,3712]{2,1,0:T(8,128)}) fusion(f32[8,3712]{1,0:T(8,128)} %get-tuple-element.14, f32[1,8,3712]{2,1,0:T(8,128)S(1)} %copy-done.1, f32[1,8,3712]{2,1,0:T(8,128)S(1)} %copy-done.2, f32[]{:T(128)} %bitcast.27, f32[1,8,3712]{2,1,0:T(8,128)S(1)} %copy-done), kind=kLoop, calls=%fused_computation.7 | loop fusion | flops 326656 | bytes 831492 | tf_op jit(solution)/shard_map/broadcast_in_dim | solution.py:525
  93.1 0.7 fusion.8
  93.8 0.6 copy.34
  94.5 0.6 copy.35
  95.1 0.6 copy.36
  (5 shorter events, 0.0 us)
Async XLA Ops:
  0.6 90.7 %copy-start = (f32[1,8,3712]{2,1,0:T(8,128)S(1)}, f32[1,8,3712]{2,1,0:T(8,128)}, u32[]{:S(2)}) copy-start(f32[1,8,3712]{2,1,0:T(8,128)} %core_hbm.1) | copy-start | bytes 356356
  0.6 93.1 %copy-start.3 = (f32[1,19,256]{2,0,1:T(1,128)S(1)}, f32[1,19,256]{2,0,1:T(1,128)}, u32[]{:S(2)}) copy-start(f32[1,19,256]{2,0,1:T(1,128)} %param.26) | copy-start | bytes 58372
  0.7 90.7 %copy-start.1 = (f32[1,8,3712]{2,1,0:T(8,128)S(1)}, f32[1,8,3712]{2,1,0:T(8,128)}, u32[]{:S(2)}) copy-start(f32[1,8,3712]{2,1,0:T(8,128)} %param.25) | copy-start | bytes 356356
  0.7 90.7 %copy-start.2 = (f32[1,8,3712]{2,1,0:T(8,128)S(1)}, f32[1,8,3712]{2,1,0:T(8,128)}, u32[]{:S(2)}) copy-start(f32[1,8,3712]{2,1,0:T(8,128)} %param.24) | copy-start | bytes 356356
  0.7 93.1 %copy-start.4 = (f32[1,19,256]{2,0,1:T(1,128)S(1)}, f32[1,19,256]{2,0,1:T(1,128)}, u32[]{:S(2)}) copy-start(f32[1,19,256]{2,0,1:T(1,128)} %param.27) | copy-start | bytes 58372
  0.7 93.1 %copy-start.5 = (f32[1,19,256]{2,0,1:T(1,128)S(1)}, f32[1,19,256]{2,0,1:T(1,128)}, u32[]{:S(2)}) copy-start(f32[1,19,256]{2,0,1:T(1,128)} %param.28) | copy-start | bytes 58372

commit v2 on v1

v2 whole, which is shorter than its diff:
```python
import functools

import jax
import jax.numpy as jnp
from jax import lax
from jax.experimental import pallas as pl
from jax.experimental.pallas import tpu as pltpu
from jax.sharding import PartitionSpec as P

MESH = pl.DeviceIdType.MESH
F32 = jnp.float32
BF16 = jnp.bfloat16
SLOTS = 8
PAD = 128
CHUNKS = 4

gamma_rate = 0.99
baseline_cost = 0.5
entropy_cost = 0.05
beta_first = 0.9
beta_second = 0.99
adam_eps = 1e-08


def dot(left, right, dims=((1,), (0,)), precision=None):
    return lax.dot_general(left, right, (dims, ((), ())), precision=precision, preferred_element_type=F32)


def bounds(total, parts, unit=128):
    units = -(-total // unit)
    return [min(total, unit * (units * i // parts)) for i in range(parts + 1)]


def turned(x):
    return x.swapaxes(1, 2)


def column(row_vector, sublanes):
    return jnp.broadcast_to(row_vector, (sublanes, row_vector.shape[1]))


def trace_gradient(out, boot, actions, done, rewards, behaviour, actions_total, steps):
    rows, frames = out.shape
    scale = 1.0 / steps
    row = lax.broadcasted_iota(jnp.int32, (rows, frames), 0)
    time = lax.broadcasted_iota(jnp.int32, (8, frames), 1) % steps
    is_logit = row < actions_total
    values = column(out[actions_total : actions_total + 1, :], 8)
    total = jnp.sum(jnp.where(is_logit, jnp.exp(out), 0.0), 0, keepdims=True)
    logp = out - jnp.log(total)
    probs = jnp.where(is_logit, jnp.exp(logp), 0.0)
    chosen = (row.astype(F32) == actions).astype(F32)
    logp_act = jnp.sum(jnp.where(is_logit, logp, 0.0) * chosen, 0, keepdims=True)
    entropy = -jnp.sum(probs * jnp.where(is_logit, logp, 0.0), 0, keepdims=True)
    ratio = column(jnp.minimum(1.0, jnp.exp(logp_act - behaviour)), 8)
    discount = column(gamma_rate * (1.0 - done), 8)
    rewards, boot = column(rewards, 8), column(boot, 8)
    last = time == steps - 1

    def later(x, by):
        return pltpu.roll(x, frames - by, 1)

    next_values = jnp.where(last, boot, later(values, 1))
    corr = ratio * (rewards + discount * next_values - values)
    factor = discount * ratio
    by = 1
    while by < steps:
        inside = time < steps - by
        corr, factor = (
            corr + factor * jnp.where(inside, later(corr, by), 0.0),
            factor * jnp.where(inside, later(factor, by), 0.0),
        )
        by *= 2
    targets = values + corr
    next_targets = jnp.where(last, boot, later(targets, 1))
    advantage = ratio * (rewards + discount * next_targets - values)
    grad_logits = scale * (
        -advantage[:1] * (chosen - probs) + entropy_cost * probs * (logp + entropy)
    )
    grad_value = scale * (-baseline_cost * (targets - values))[:1]
    return jnp.where(is_logit, grad_logits, jnp.where(row == actions_total, grad_value, 0.0))


def step_kernel(
    sizes,
    learn_hbm, own_hbm, opp_hbm, opponent_hbm, actions_hbm, done_hbm, rewards_hbm, behaviour_hbm, core_hbm, head_hbm,
    grad_out, head_out, own_out, opp_out,
    x, own, opp, opponent, actions, done, rewards, behaviour, core, head,
    shards, weights, mine, for_sibling, from_sibling, sums_out, sums_in, frames_out, frames_in,
    played_out, played_in, heads, head_part, head_from, head_all, head_final,
    load_sem, gather_send, gather_recv, pair_send, pair_recv, own_send, own_recv,
    frame_send, frame_recv, played_send, played_recv, reduce_send, reduce_recv,
    half_send, half_recv, hring_send, hring_recv, hpair_send, hpair_recv, hlast_send, hlast_recv,
):
    (agents, chips, shard, envs, steps, feat, units, head_rows, agent_y) = sizes
    frames = envs * steps
    width = feat + units
    acts = head_rows - 1
    edges = bounds(width, CHUNKS)
    far = chips // 2
    half = CHUNKS // 2
    stages = far // 2
    agent, dp = lax.axis_index("agent"), lax.axis_index("dp")
    chip, side = dp // 2, dp % 2
    other = 1 - side
    agent_x = agents // agent_y
    ax, ay = agent // agent_y, agent % agent_y

    def chip_at(offset):
        return lax.rem(chip + (offset + 2 * chips), chips)

    sibling = (agent, 2 * chip + other)
    sign = [1, -1]
    next_one = [(agent, 2 * chip_at(k) + side) for k in sign]
    next_two = [(agent, 2 * chip_at(2 * k) + side) for k in sign]
    target = [next_two, next_one]
    shifts = [(i, j) for i in range(agent_x) for j in range(agent_y) if (i, j) != (0, 0)]
    to_agent = [lax.rem(ax + i, agent_x) * agent_y + lax.rem(ay + j, agent_y) for i, j in shifts]
    from_agent = [lax.rem(ax + agent_x - i, agent_x) * agent_y + lax.rem(ay + agent_y - j, agent_y) for i, j in shifts]

    barrier = pltpu.get_barrier_semaphore()
    peers = [sibling, *next_one, *next_two, *[(a, dp) for a in to_agent]]
    for peer in peers:
        pl.semaphore_signal(barrier, inc=1, device_id=peer, device_id_type=MESH)

    loads = [
        pltpu.make_async_copy(src, dst, load_sem.at[i])
        for i, (src, dst) in enumerate((
            (core_hbm.at[0], core), (head_hbm, head), (opponent_hbm.at[0], opponent), (opp_hbm.at[0], opp),
            (learn_hbm.at[0], x), (own_hbm.at[0], own), (actions_hbm.at[0], actions), (done_hbm.at[0], done),
            (rewards_hbm.at[0], rewards), (behaviour_hbm.at[0], behaviour),
        ))
    ]
    for load in loads:
        load.start()

    def cols(f):
        return pl.ds(edges[f], edges[f + 1] - edges[f])

    def remote(src, dst, send, recv, to):
        return pltpu.make_async_remote_copy(
            src_ref=src, dst_ref=dst, send_sem=send, recv_sem=recv, device_id=to, device_id_type=MESH
        )

    kinds = (0, 1)

    def gather_has(way, kind, i, f):
        return kind == 1 or i < stages - 1 or (f < half) == (way == 0)

    def gather(way, kind, i, f):
        block = shards.at[chip_at(-sign[way] * 2 * i), side, :, cols(f)]
        at = (way, kind, i, f)
        return remote(block, block, gather_send.at[at], gather_recv.at[at], target[kind][way])

    def came_from(way, kind, i):
        return chip_at(-sign[way] * (2 * i + 2 - kind))

    def gathered(way, kind, i, f):
        block = shards.at[came_from(way, kind, i), side, :, cols(f)]
        at = (way, kind, i, f)
        return remote(block, block, gather_send.at[at], gather_recv.at[at], target[kind][way])

    def pair(way, kind, i, f, which):
        block = shards.at[came_from(way, kind, i), which, :, cols(f)]
        at = (way, kind, i, f)
        return remote(block, block, pair_send.at[at], pair_recv.at[at], sibling)

    def own_pair(which):
        block = shards.at[chip, which]
        return remote(block, block, own_send, own_recv, sibling)

    loads[2].wait()
    ids = opponent[...]
    agent_row = lax.broadcasted_iota(jnp.int32, (PAD, envs), 0)
    member = (ids == agent_row).astype(F32)
    before = (
        lax.broadcasted_iota(jnp.int32, (envs, envs), 0) < lax.broadcasted_iota(jnp.int32, (envs, envs), 1)
    ).astype(BF16)
    ranks = jnp.sum(dot(member.astype(BF16), before) * member, 0, keepdims=True)
    position = ids * SLOTS + ranks.astype(jnp.int32)
    slot_row = lax.broadcasted_iota(jnp.int32, (agents * SLOTS, envs), 0)
    placed = (position == slot_row).astype(BF16)
    loads[0].wait()
    shards[chip, side] = core[...].astype(BF16)
    loads[3].wait()
    frames_out[...] = dot(placed, opp[...]).reshape(agents, SLOTS, feat).astype(BF16)

    pl.semaphore_wait(barrier, len(peers))
    for kind in kinds:
        for f in range(CHUNKS):
            for way in (0, 1):
                if gather_has(way, kind, 0, f):
                    gather(way, kind, 0, f).start()
    own_pair(side).start()

    def send_frames(i):
        return remote(
            frames_out.at[to_agent[i]], frames_in.at[agent], frame_send.at[i], frame_recv.at[i], (to_agent[i], dp)
        )

    def frames_come(i):
        return remote(
            frames_out.at[to_agent[i]], frames_in.at[from_agent[i]], frame_send.at[i], frame_recv.at[i], (to_agent[i], dp)
        )

    for i in range(len(shifts)):
        send_frames(i).start()
    frames_in[agent] = frames_out[agent]

    loads[1].wait()
    heads[...] = jnp.zeros_like(heads)
    for i in range(head_rows):
        heads[i : i + 1, :] = head[i]
    head_bf = heads[...].astype(BF16)
    head_turned = heads[...].T.astype(BF16)
    small = head_bf[:32]

    for load in loads[6:]:
        load.wait()
    stacked = jnp.concatenate(
        [actions[...].astype(F32), done[...].astype(F32), rewards[...], behaviour[...]], 0
    )
    env_lane = lax.broadcasted_iota(jnp.int32, (envs, frames), 1)
    to_frames = (env_lane // steps == lax.broadcasted_iota(jnp.int32, (envs, frames), 0)).astype(F32)
    spread = dot(stacked, to_frames, precision=lax.Precision.HIGHEST).reshape(4, steps, frames)
    same_step = (
        lax.broadcasted_iota(jnp.int32, (steps, frames), 1) % steps
        == lax.broadcasted_iota(jnp.int32, (steps, frames), 0)
    )
    flat = jnp.sum(jnp.where(same_step[None], spread, 0.0), 1)

    loads[4].wait()
    loads[5].wait()

    def repack(at, f):
        pair_of = [shards[at, k, :, cols(f)].astype(F32) for k in (0, 1)]
        weights[at, :, cols(f)] = jnp.concatenate(pair_of, 0).astype(BF16)

    def weight_cols(lo, hi):
        return weights[:, :, lo:hi].reshape(units, hi - lo)

    def frame_cols(lo, hi):
        return x[:, :, lo:hi].reshape(frames, hi - lo)

    def layer_one(f, total, own_total):
        lo, hi = edges[f], min(edges[f + 1], feat)
        if lo >= hi:
            return total, own_total
        part = weight_cols(lo, hi)
        one = dot(part, frame_cols(lo, hi), ((1,), (1,)))
        two = dot(own[:, lo:hi], part, ((1,), (1,)))
        return (one, two) if total is None else (total + one, own_total + two)

    total, own_total = None, None

    def forwarded(i, f):
        for kind in kinds:
            for way in (0, 1):
                if gather_has(way, kind, i, f):
                    pair(way, kind, i, f, other).wait_recv()
                    repack(came_from(way, kind, i), f)

    for i in range(stages):
        for f in range(CHUNKS):
            for kind in kinds:
                for way in (0, 1):
                    if gather_has(way, kind, i, f):
                        gathered(way, kind, i, f).wait_recv()
                        if kind == 0 and i + 1 < stages:
                            for later in kinds:
                                if gather_has(way, later, i + 1, f):
                                    gather(way, later, i + 1, f).start()
                        pair(way, kind, i, f, side).start()
            if i == 0:
                if f == 0:
                    own_pair(other).wait_recv()
                repack(chip, f)
            else:
                forwarded(i - 1, f)
            if i == stages - 1 and f > 0:
                forwarded(i, f - 1)
                total, own_total = layer_one(f - 1, total, own_total)
    forwarded(stages - 1, CHUNKS - 1)
    total, own_total = layer_one(CHUNKS - 1, total, own_total)

    second = weight_cols(feat, width)
    second_turned = second.astype(F32).T.astype(BF16)

    def narrow(first):
        act = jnp.maximum(first, 0.0)
        late = dot(act.astype(BF16), second, ((1,), (1,)))
        act = jnp.maximum(late, 0.0) + act
        return dot(head_bf, act.astype(BF16), ((1,), (1,)))

    own_net = narrow(own_total)
    own_out[...] = own_net[:32]
    boot = dot(column(own_net[acts : acts + 1], 8), to_frames, precision=lax.Precision.HIGHEST)[:1]

    act_one = jnp.maximum(total, 0.0)
    one_bf = act_one.astype(BF16)
    pre_two = dot(second, one_bf)
    two_bf = (jnp.maximum(pre_two, 0.0) + act_one).astype(BF16)
    net = dot(small, two_bf)
    out_grad = trace_gradient(net, boot, flat[0:1], flat[1:2], flat[2:3], flat[3:4], acts, steps).astype(BF16)

    head_grad = dot(out_grad, two_bf, ((1,), (1,)))
    half_units = units // 2
    for k in (0, 1):
        head_part[k] = head_grad[:, k * half_units : (k + 1) * half_units].astype(BF16)
    hpair = remote(head_part.at[other], head_from, hpair_send, hpair_recv, sibling)
    hpair.start()

    g_two = dot(head_turned[:, :32], out_grad)
    gp_two = jnp.where(pre_two > 0, g_two, 0.0).astype(BF16)
    g_one = g_two + dot(second_turned, gp_two)
    gp_one = jnp.where(total > 0, g_one, 0.0).astype(BF16)

    hpair.wait_recv()
    head_all[chip] = (head_part[side].astype(F32) + head_from[...].astype(F32)).astype(BF16)

    def head_has(way, kind, i):
        return kind == 1 or i < stages - 1 or way == 0

    def head_ring(way, kind, i):
        block = head_all.at[chip_at(-sign[way] * 2 * i)]
        at = (way, kind, i)
        return remote(block, block, hring_send.at[at], hring_recv.at[at], target[kind][way])

    def head_come(way, kind, i):
        block = head_all.at[came_from(way, kind, i)]
        at = (way, kind, i)
        return remote(block, block, hring_send.at[at], hring_recv.at[at], target[kind][way])

    def head_step(i):
        for kind in kinds:
            for way in (0, 1):
                if head_has(way, kind, i):
                    head_come(way, kind, i).wait_recv()
                    if kind == 0 and i + 1 < stages:
                        for later in kinds:
                            if head_has(way, later, i + 1):
                                head_ring(way, later, i + 1).start()

    for kind in kinds:
        for way in (0, 1):
            if head_has(way, kind, 0):
                head_ring(way, kind, 0).start()

    def swap(f):
        return remote(
            for_sibling.at[:, :, cols(f)], from_sibling.at[:, :, cols(f)], half_send.at[f], half_recv.at[f], sibling
        )

    first_side = side == 0
    for f in range(CHUNKS):
        lo, hi = edges[f], edges[f + 1]
        parts = []
        if lo < feat:
            parts.append(dot(gp_one, frame_cols(lo, min(hi, feat))))
        if hi > feat:
            parts.append(dot(gp_two, one_bf, ((1,), (1,))))
        grad = parts[0] if len(parts) == 1 else jnp.concatenate(parts, 1)
        grad = grad.reshape(chips, 2, shard, hi - lo)
        for_sibling[:, :, lo:hi] = jnp.where(first_side, grad[:, 1], grad[:, 0]).astype(BF16)
        swap(f).start()
        mine[:, :, lo:hi] = jnp.where(first_side, grad[:, 0], grad[:, 1])

    def reduce_has(way, kind, i, f):
        return kind == 1 or i > 0 or (f < half) == (way == 0)

    def reduce_to(way, kind, i, f):
        at = (way, kind, i)
        return remote(
            sums_out.at[(*at, slice(None), cols(f))], sums_in.at[(*at, slice(None), cols(f))],
            reduce_send.at[(*at, f)], reduce_recv.at[(*at, f)], target[kind][way],
        )

    def arrived(way, i, f, term):
        for kind in kinds:
            if reduce_has(way, kind, i, f):
                reduce_to(way, kind, i, f).wait_recv()
                term = term + sums_in[way, kind, i, :, cols(f)].astype(F32)
        return term

    def reduce_step(way, i, f):
        for kind in kinds:
            if reduce_has(way, kind, i, f):
                term = mine[chip_at(sign[way] * (far - 2 * i - kind)), :, cols(f)]
                if kind == 0 and i > 0:
                    term = arrived(way, i - 1, f, term)
                sums_out[way, kind, i, :, cols(f)] = term.astype(BF16)
                reduce_to(way, kind, i, f).start()

    for f in range(CHUNKS):
        swap(f).wait_recv()
        lo, hi = edges[f], edges[f + 1]
        mine[:, :, lo:hi] = mine[:, :, lo:hi] + from_sibling[:, :, lo:hi].astype(F32)
        for way in (0, 1):
            reduce_step(way, 0, f)

    def play():
        for i in range(len(shifts)):
            frames_come(i).wait_recv()
        came = frames_in[...].astype(F32).reshape(agents * SLOTS, feat).astype(BF16)
        act = jnp.maximum(dot(came, weight_cols(0, feat), ((1,), (1,))), 0.0)
        late = dot(act.astype(BF16), second, ((1,), (1,)))
        act = jnp.maximum(late, 0.0) + act
        answers = dot(act.astype(BF16), head_bf, ((1,), (1,)))
        played_out[...] = answers.reshape(agents, SLOTS, PAD).astype(BF16)
        for i in range(len(shifts)):
            remote(
                played_out.at[to_agent[i]], played_in.at[agent], played_send.at[i], played_recv.at[i], (to_agent[i], dp)
            ).start()
        played_in[agent] = played_out[agent]

    play()
    for i in range(1, stages):
        head_step(i - 1)
        for f in range(CHUNKS):
            for way in (0, 1):
                reduce_step(way, i, f)

    head_step(stages - 1)
    head_final[side] = jnp.sum(head_all[...].astype(F32), 0)
    hlast = remote(head_final.at[side], head_final.at[side], hlast_send, hlast_recv, sibling)
    hlast.start()

    def played_come(i):
        return remote(
            played_out.at[to_agent[i]], played_in.at[from_agent[i]], played_send.at[i], played_recv.at[i], (to_agent[i], dp)
        )

    for i in range(len(shifts)):
        played_come(i).wait_recv()
    back = played_in[...].astype(F32).reshape(agents * SLOTS, PAD).T.astype(BF16)
    opp_out[...] = dot(back, placed)[:32].astype(BF16)

    for f in range(CHUNKS):
        total = mine[chip, :, cols(f)]
        for way in (0, 1):
            total = arrived(way, stages - 1, f, total)
        grad_out[:, cols(f)] = total

    remote(head_final.at[other], head_final.at[other], hlast_send, hlast_recv, sibling).wait_recv()
    head_out[...] = head_final[...]

    for i in range(stages):
        for kind in kinds:
            for way in (0, 1):
                for f in range(CHUNKS):
                    if gather_has(way, kind, i, f):
                        gather(way, kind, i, f).wait_send()
                        pair(way, kind, i, f, side).wait_send()
                    if reduce_has(way, kind, i, f):
                        reduce_to(way, kind, i, f).wait_send()
                if head_has(way, kind, i):
                    head_ring(way, kind, i).wait_send()
    own_pair(side).wait_send()
    hpair.wait_send()
    hlast.wait_send()
    for f in range(CHUNKS):
        swap(f).wait_send()
    for i in range(len(shifts)):
        send_frames(i).wait_send()
        played_come(i).wait_send()


def adam_step(master, moment, second, grad, rate):
    moment = beta_first * moment + (1.0 - beta_first) * grad
    second = beta_second * second + (1.0 - beta_second) * grad * grad
    master = master - rate * moment / (jnp.sqrt(second) + adam_eps)
    return (master, moment, second)


def finish_kernel(
    head_rows, rate, grad, head_grad, own_net, opp_net, core, core_mom, core_vel, head, head_mom, head_vel,
    own_out, opp_out, new_core, new_mom, new_vel, new_head, new_head_mom, new_head_vel,
):
    by = rate[0]
    new_core[0], new_mom[0], new_vel[0] = adam_step(core[0], core_mom[0], core_vel[0], grad[...], by)
    for i in range(head_rows):
        row = jnp.concatenate([head_grad[0, i : i + 1], head_grad[1, i : i + 1]], 1)
        new_head[i], new_head_mom[i], new_head_vel[i] = adam_step(head[i], head_mom[i], head_vel[i], row, by)
    for i in range(head_rows - 1):
        own_out[i] = own_net[i : i + 1]
    opp_out[0] = opp_net[0 : head_rows - 1]


def per_device(
    learn_obs, own_obs, opp_obs, opponent, actions, done, rewards, behaviour,
    core_master, core_mom, core_vel, head_master, head_mom, head_vel, rates,
):
    _, envs, steps, feat = learn_obs.shape
    _, shard, width = core_master.shape
    _, head_rows, units = head_master.shape
    agents, dp = lax.axis_size("agent"), lax.axis_size("dp")
    chips = dp // 2
    far = chips // 2
    stages = far // 2
    agent_y = 4 if agents % 4 == 0 else agents
    sizes = (agents, chips, shard, envs, steps, feat, units, head_rows, agent_y)
    vmem, dma = pltpu.VMEM, pltpu.SemaphoreType.DMA
    shifts = max(1, agents - 1)
    anywhere = pl.BlockSpec(memory_space=pl.ANY)
    in_vmem = pl.BlockSpec(memory_space=vmem)
    head_rows_first = [a.swapaxes(0, 1) for a in (head_master, head_mom, head_vel)]
    grad, head_grad, own_net, opp_net = pl.pallas_call(
        functools.partial(step_kernel, sizes),
        out_shape=(
            jax.ShapeDtypeStruct((shard, width), F32),
            jax.ShapeDtypeStruct((2, 32, units // 2), F32),
            jax.ShapeDtypeStruct((32, envs), F32),
            jax.ShapeDtypeStruct((32, envs), BF16),
        ),
        in_specs=[anywhere] * 10,
        out_specs=(in_vmem,) * 4,
        scratch_shapes=[
            vmem((envs, steps, feat), BF16),
            vmem((envs, feat), BF16),
            vmem((envs, feat), BF16),
            vmem((1, envs), jnp.int32),
            vmem((steps, envs), jnp.int32),
            vmem((steps, envs), jnp.int32),
            vmem((steps, envs), F32),
            vmem((steps, envs), F32),
            vmem((shard, width), F32),
            vmem((head_rows, 1, units), F32),
            vmem((chips, 2, shard, width), BF16),
            vmem((chips, 2 * shard, width), BF16),
            vmem((chips, shard, width), F32),
            vmem((chips, shard, width), BF16),
            vmem((chips, shard, width), BF16),
            vmem((2, 2, stages, shard, width), BF16),
            vmem((2, 2, stages, shard, width), BF16),
            vmem((agents, SLOTS, feat), BF16),
            vmem((agents, SLOTS, feat), BF16),
            vmem((agents, SLOTS, PAD), BF16),
            vmem((agents, SLOTS, PAD), BF16),
            vmem((PAD, units), F32),
            vmem((2, 32, units // 2), BF16),
            vmem((32, units // 2), BF16),
            vmem((chips, 32, units // 2), BF16),
            vmem((2, 32, units // 2), F32),
            dma((10,)),
            dma((2, 2, stages, CHUNKS)),
            dma((2, 2, stages, CHUNKS)),
            dma((2, 2, stages, CHUNKS)),
            dma((2, 2, stages, CHUNKS)),
            dma,
            dma,
            dma((shifts,)),
            dma((shifts,)),
            dma((shifts,)),
            dma((shifts,)),
            dma((2, 2, stages, CHUNKS)),
            dma((2, 2, stages, CHUNKS)),
            dma((CHUNKS,)),
            dma((CHUNKS,)),
            dma((2, 2, stages)),
            dma((2, 2, stages)),
            dma,
            dma,
            dma,
            dma,
        ],
        compiler_params=pltpu.CompilerParams(
            collective_id=0, has_side_effects=True, vmem_limit_bytes=56 * 2**20
        ),
    )(
        learn_obs, own_obs, opp_obs, turned(opponent), turned(actions), turned(done), turned(rewards), turned(behaviour),
        core_master, head_rows_first[0],
    )
    own_logits, opp_logits, *new = pl.pallas_call(
        functools.partial(finish_kernel, head_rows),
        out_shape=(
            jax.ShapeDtypeStruct((head_rows - 1, 1, envs), F32),
            jax.ShapeDtypeStruct((1, head_rows - 1, envs), BF16),
            *[jax.ShapeDtypeStruct((1, shard, width), F32)] * 3,
            *[jax.ShapeDtypeStruct((head_rows, 1, units), F32)] * 3,
        ),
        in_specs=[pl.BlockSpec(memory_space=pltpu.SMEM)] + [in_vmem] * 10,
        out_specs=(in_vmem,) * 8,
        compiler_params=pltpu.CompilerParams(vmem_limit_bytes=8 * 2**20),
    )(rates, grad, head_grad, own_net, opp_net, core_master, core_mom, core_vel, *head_rows_first)
    return (
        own_logits.transpose(1, 2, 0),
        turned(opp_logits),
        *new[:3],
        *[a.swapaxes(0, 1) for a in new[3:]],
    )


def solution(mesh):
    rows, whole = P("agent", "dp"), P("agent")
    return jax.shard_map(
        per_device,
        mesh=mesh,
        in_specs=(rows,) * 11 + (whole,) * 4,
        out_specs=(rows,) * 5 + (whole,) * 3,
        check_vma=False,
    )
```

time: 96.3 us -> 70.3 us (0.73)
  Pallas kernels: 78.9 us -> 65.4 us
  local copies, waits for them, and re-layouts: 13.7 us -> 3.09 us
  other arithmetic: 1.74 us -> 0 us
    pallas_call x1, Pallas kernels: 78.9 us -> 64.5 us  [per_device(): pl.pallas_call(functools.partial(step_kernel, sizes), out_shape=(jax.Shap...]
    unnamed x23 -> x20, local copies, waits for them, and re-layouts: 11.5 us -> 3.09 us
    broadcast_in_dim x1 -> x0, other arithmetic: 1.7 us -> none  [per_device(): a[None]]
    broadcast_in_dim x2 -> x0, local copies, waits for them, and re-layouts: 1.42 us -> none  [the longest x1 0.72 us: per_device(): own_net[None, :, :head_rows - 1]]
where the time goes in v2:
time: 70.3 us; the launch traced here: 70 us
  Pallas kernels  65.4 us (93%)
  local copies, waits for them, and re-layouts  3.09 us (4%)
  between operations  1.48 us (2%)
    pallas_call x1, Pallas kernels, per_device(): pl.pallas_call(functools.partial(step_kernel, sizes), out_shape=(jax.Shap...  64.5 us
    unnamed x20, local copies, waits for them, and re-layouts  3.09 us

profile of v2, /device:TPU:1, one launch (start us, length us, event | category | flops | bytes accessed | tf_op | source)
XLA Modules:
  0.0 70.0 jit_solution(3223692260368189911)
XLA Ops:
  0.6 0.0 copy-start
  0.6 0.0 copy-start.7
  0.7 0.0 copy-start.6
  0.7 0.0 copy-start.4
  0.7 0.0 copy-start.2
  0.7 0.0 copy-start.1
  1.4 64.5 %shard_map.206 = (f32[8,3712]{1,0:T(8,128)}, f32[2,32,128]{2,1,0:T(8,128)}, f32[32,32]{1,0:T(8,128)}, bf16[32,32]{1,0:T(8,128)(2,1)}) custom-call(bf16[1,32,16,3456]{3,2,1,0:T(8,128)(2,1)} %learn_hbm.1, bf16[1,32,3456]{2,1,0:T(8,128)(2,1)} %own_hbm.1, bf16[1,32,3456]{2,1,0:T(8,128)(2,1)} %opp_hbm.1, s32[1,1,32]{2,1,0:T(1,128)} %bitcast.21, ...), custom_call_target="tpu_custom_call" | custom-call | tf_op jit(solution)/shard_map/pallas_call | solution.py:507
  66.0 0.0 copy-done
  66.0 0.0 copy-done.7
  66.0 0.0 copy-done.6
  66.0 0.0 copy-done.4
  66.0 0.0 copy-done.2
  66.0 0.0 copy-done.1
  66.0 0.0 copy-start.3
  66.1 0.9 %copy-done.3 = f32[8,3712]{1,0:T(8,128)S(1)} copy-done((f32[8,3712]{1,0:T(8,128)S(1)}, f32[8,3712]{1,0:T(8,128)}, u32[]{:S(2)}) %copy-start.3) | copy-done | bytes 118808
  66.9 0.0 copy-start.5
  66.9 0.8 %copy-done.5 = f32[2,32,128]{2,1,0:T(8,128)S(1)} copy-done((f32[2,32,128]{2,1,0:T(8,128)S(1)}, f32[2,32,128]{2,1,0:T(8,128)}, u32[]{:S(2)}) %copy-start.5) | copy-done | bytes 32792
  67.7 0.0 copy-start.8
  67.7 0.7 %copy-done.8 = f32[32,32]{1,0:T(8,128)S(1)} copy-done((f32[32,32]{1,0:T(8,128)S(1)}, f32[32,32]{1,0:T(8,128)}, u32[]{:S(2)}) %copy-start.8) | copy-done | bytes 4120
  68.4 0.0 copy-start.9
  68.4 0.7 copy-done.9
  69.1 0.8 %shard_map.207 = (f32[18,1,32]{2,1,0:T(1,128)}, bf16[1,18,32]{2,1,0:T(8,128)(2,1)}, f32[1,8,3712]{2,1,0:T(8,128)}, f32[1,8,3712]{2,1,0:T(8,128)}, f32[1,8,3712]{...) custom-call(f32[1]{0:T(128)S(6)} %copy.23.rate, f32[8,3712]{1,0:T(8,128)S(1)} %copy-done.3, ...), custom_call_target="tpu_custom_call" | custom-call | tf_op jit(solution)/shard_map/pallas_call | solution.py:573
Async XLA Ops:
  0.6 65.3 %copy-start = (f32[1,8,3712]{2,1,0:T(8,128)S(1)}, f32[1,8,3712]{2,1,0:T(8,128)}, u32[]{:S(2)}) copy-start(f32[1,8,3712]{2,1,0:T(8,128)} %core.1) | copy-start | bytes 356356
  0.6 65.3 %copy-start.7 = (f32[1,19,256]{2,0,1:T(1,128)S(1)}, f32[1,19,256]{2,0,1:T(1,128)}, u32[]{:S(2)}) copy-start(f32[1,19,256]{2,0,1:T(1,128)} %param.28) | copy-start | bytes 58372
  0.7 65.3 %copy-start.6 = (f32[1,19,256]{2,0,1:T(1,128)S(1)}, f32[1,19,256]{2,0,1:T(1,128)}, u32[]{:S(2)}) copy-start(f32[1,19,256]{2,0,1:T(1,128)} %param.27) | copy-start | bytes 58372
  0.7 65.3 %copy-start.4 = (f32[1,19,256]{2,0,1:T(1,128)S(1)}, f32[1,19,256]{2,0,1:T(1,128)}, u32[]{:S(2)}) copy-start(f32[1,19,256]{2,0,1:T(1,128)} %param.26) | copy-start | bytes 58372
  0.7 65.3 %copy-start.2 = (f32[1,8,3712]{2,1,0:T(8,128)S(1)}, f32[1,8,3712]{2,1,0:T(8,128)}, u32[]{:S(2)}) copy-start(f32[1,8,3712]{2,1,0:T(8,128)} %core_vel.1) | copy-start | bytes 356356
  0.7 65.3 %copy-start.1 = (f32[1,8,3712]{2,1,0:T(8,128)S(1)}, f32[1,8,3712]{2,1,0:T(8,128)}, u32[]{:S(2)}) copy-start(f32[1,8,3712]{2,1,0:T(8,128)} %core_mom.1) | copy-start | bytes 356356
  66.0 0.9 %copy-start.3 = (f32[8,3712]{1,0:T(8,128)S(1)}, f32[8,3712]{1,0:T(8,128)}, u32[]{:S(2)}) copy-start(f32[8,3712]{1,0:T(8,128)} %get-tuple-element.20.grad) | copy-start | bytes 356356
  66.9 0.8 %copy-start.5 = (f32[2,32,128]{2,1,0:T(8,128)S(1)}, f32[2,32,128]{2,1,0:T(8,128)}, u32[]{:S(2)}) copy-start(f32[2,32,128]{2,1,0:T(8,128)} %get-tuple-element.21.head_grad) | copy-start | bytes 98308
  67.7 0.7 %copy-start.8 = (f32[32,32]{1,0:T(8,128)S(1)}, f32[32,32]{1,0:T(8,128)}, u32[]{:S(2)}) copy-start(f32[32,32]{1,0:T(8,128)} %get-tuple-element.22.own_net) | copy-start | bytes 12292
  68.4 0.7 copy-start.9

commit v3 on v2

--- a/solution.py
+++ b/solution.py
@@ -12,7 +12,7 @@
 BF16 = jnp.bfloat16
 SLOTS = 8
 PAD = 128
-CHUNKS = 4
+CHUNKS = 3
 
 gamma_rate = 0.99
 baseline_cost = 0.5
@@ -86,8 +86,8 @@
     learn_hbm, own_hbm, opp_hbm, opponent_hbm, actions_hbm, done_hbm, rewards_hbm, behaviour_hbm, core_hbm, head_hbm,
     grad_out, head_out, own_out, opp_out,
     x, own, opp, opponent, actions, done, rewards, behaviour, core, head,
-    shards, weights, mine, for_sibling, from_sibling, sums_out, sums_in, frames_out, frames_in,
-    played_out, played_in, heads, head_part, head_from, head_all, head_final,
+    shards, weights, mine, for_sibling, from_sibling, sums_out, sums_in, frames_out, frames_mid, frames_in,
+    played_out, played_mid, played_in, heads, head_part, head_from, head_all, head_final,
     load_sem, gather_send, gather_recv, pair_send, pair_recv, own_send, own_recv,
     frame_send, frame_recv, played_send, played_recv, reduce_send, reduce_recv,
     half_send, half_recv, hring_send, hring_recv, hpair_send, hpair_recv, hlast_send, hlast_recv,
@@ -114,12 +114,15 @@
     next_one = [(agent, 2 * chip_at(k) + side) for k in sign]
     next_two = [(agent, 2 * chip_at(2 * k) + side) for k in sign]
     target = [next_two, next_one]
-    shifts = [(i, j) for i in range(agent_x) for j in range(agent_y) if (i, j) != (0, 0)]
-    to_agent = [lax.rem(ax + i, agent_x) * agent_y + lax.rem(ay + j, agent_y) for i, j in shifts]
-    from_agent = [lax.rem(ax + agent_x - i, agent_x) * agent_y + lax.rem(ay + agent_y - j, agent_y) for i, j in shifts]
+    x_to = [lax.rem(ax + i, agent_x) for i in range(1, agent_x)]
+    x_from = [lax.rem(ax + agent_x - i, agent_x) for i in range(1, agent_x)]
+    y_to = [lax.rem(ay + i, agent_y) for i in range(1, agent_y)]
+    y_from = [lax.rem(ay + agent_y - i, agent_y) for i in range(1, agent_y)]
+    x_peer = [(k * agent_y + ay, dp) for k in x_to]
+    y_peer = [(ax * agent_y + k, dp) for k in y_to]
 
     barrier = pltpu.get_barrier_semaphore()
-    peers = [sibling, *next_one, *next_two, *[(a, dp) for a in to_agent]]
+    peers = [*next_two, *next_one, *x_peer, *y_peer, sibling]
     for peer in peers:
         pl.semaphore_signal(barrier, inc=1, device_id=peer, device_id_type=MESH)
 
@@ -168,6 +171,17 @@
     def own_pair(which):
         block = shards.at[chip, which]
         return remote(block, block, own_send, own_recv, sibling)
+
+    loads[0].wait()
+    shards[chip, side] = core[...].astype(BF16)
+
+    pl.semaphore_wait(barrier, len(peers))
+    for kind in kinds:
+        for f in range(CHUNKS):
+            for way in (0, 1):
+                if gather_has(way, kind, 0, f):
+                    gather(way, kind, 0, f).start()
+    own_pair(side).start()
 
     loads[2].wait()
     ids = opponent[...]
@@ -180,32 +194,28 @@
     position = ids * SLOTS + ranks.astype(jnp.int32)
     slot_row = lax.broadcasted_iota(jnp.int32, (agents * SLOTS, envs), 0)
     placed = (position == slot_row).astype(BF16)
-    loads[0].wait()
-    shards[chip, side] = core[...].astype(BF16)
     loads[3].wait()
-    frames_out[...] = dot(placed, opp[...]).reshape(agents, SLOTS, feat).astype(BF16)
-
-    pl.semaphore_wait(barrier, len(peers))
-    for kind in kinds:
-        for f in range(CHUNKS):
-            for way in (0, 1):
-                if gather_has(way, kind, 0, f):
-                    gather(way, kind, 0, f).start()
-    own_pair(side).start()
-
-    def send_frames(i):
+    frames_out[...] = dot(placed, opp[...]).reshape(agent_x, agent_y, SLOTS, feat).astype(BF16)
+
+    def frames_x(i, at):
+        return remote(frames_out.at[x_to[i]], frames_mid.at[at], frame_send.at[0, i], frame_recv.at[0, i], x_peer[i])
+
+    def frames_y(i, at):
         return remote(
-            frames_out.at[to_agent[i]], frames_in.at[agent], frame_send.at[i], frame_recv.at[i], (to_agent[i], dp)
+            frames_mid.at[:, y_to[i]], frames_in.at[:, at], frame_send.at[1, i], frame_recv.at[1, i], y_peer[i]
         )
 
-    def frames_come(i):
-        return remote(
-            frames_out.at[to_agent[i]], frames_in.at[from_agent[i]], frame_send.at[i], frame_recv.at[i], (to_agent[i], dp)
-        )
-
-    for i in range(len(shifts)):
-        send_frames(i).start()
-    frames_in[agent] = frames_out[agent]
+    for i in range(agent_x - 1):
+        frames_x(i, ax).start()
+    frames_mid[ax] = frames_out[ax]
+
+    def frames_on():
+        for i in range(agent_x - 1):
+            frames_x(i, x_from[i]).wait_recv()
+        for i in range(agent_y - 1):
+            frames_y(i, ay).start()
+        frames_in[:, ay] = frames_mid[:, ay]
+
 
     loads[1].wait()
     heads[...] = jnp.zeros_like(heads)
@@ -280,6 +290,8 @@
             if i == stages - 1 and f > 0:
                 forwarded(i, f - 1)
                 total, own_total = layer_one(f - 1, total, own_total)
+        if i == max(0, stages - 2):
+            frames_on()
     forwarded(stages - 1, CHUNKS - 1)
     total, own_total = layer_one(CHUNKS - 1, total, own_total)
 
@@ -332,14 +344,13 @@
         return remote(block, block, hring_send.at[at], hring_recv.at[at], target[kind][way])
 
     def head_step(i):
-        for kind in kinds:
-            for way in (0, 1):
-                if head_has(way, kind, i):
-                    head_come(way, kind, i).wait_recv()
-                    if kind == 0 and i + 1 < stages:
-                        for later in kinds:
-                            if head_has(way, later, i + 1):
-                                head_ring(way, later, i + 1).start()
+        for way in (0, 1):
+            if head_has(way, 0, i):
+                head_come(way, 0, i).wait_recv()
+                if i + 1 < stages:
+                    for later in kinds:
+                        if head_has(way, later, i + 1):
+                            head_ring(way, later, i + 1).start()
 
     for kind in kinds:
         for way in (0, 1):
@@ -398,40 +409,59 @@
         for way in (0, 1):
             reduce_step(way, 0, f)
 
+    def answers_y(i, at):
+        return remote(
+            played_out.at[:, y_to[i]], played_mid.at[:, at], played_send.at[0, i], played_recv.at[0, i], y_peer[i]
+        )
+
+    def answers_x(i, at):
+        return remote(
+            played_mid.at[x_to[i]], played_in.at[at], played_send.at[1, i], played_recv.at[1, i], x_peer[i]
+        )
+
     def play():
-        for i in range(len(shifts)):
-            frames_come(i).wait_recv()
+        for i in range(agent_y - 1):
+            frames_y(i, y_from[i]).wait_recv()
         came = frames_in[...].astype(F32).reshape(agents * SLOTS, feat).astype(BF16)
         act = jnp.maximum(dot(came, weight_cols(0, feat), ((1,), (1,))), 0.0)
         late = dot(act.astype(BF16), second, ((1,), (1,)))
         act = jnp.maximum(late, 0.0) + act
         answers = dot(act.astype(BF16), head_bf, ((1,), (1,)))
-        played_out[...] = answers.reshape(agents, SLOTS, PAD).astype(BF16)
-        for i in range(len(shifts)):
-            remote(
-                played_out.at[to_agent[i]], played_in.at[agent], played_send.at[i], played_recv.at[i], (to_agent[i], dp)
-            ).start()
-        played_in[agent] = played_out[agent]
-
-    play()
+        played_out[...] = answers.reshape(agent_x, agent_y, SLOTS, PAD).astype(BF16)
+        for i in range(agent_y - 1):
+            answers_y(i, ay).start()
+        played_mid[:, ay] = played_out[:, ay]
+
+    def answers_on():
+        for i in range(agent_y - 1):
+            answers_y(i, y_from[i]).wait_recv()
+        for i in range(agent_x - 1):
+            answers_x(i, ax).start()
+        played_in[ax] = played_mid[ax]
+
+    if stages == 1:
+        play()
+        answers_on()
     for i in range(1, stages):
         head_step(i - 1)
         for f in range(CHUNKS):
             for way in (0, 1):
                 reduce_step(way, i, f)
+        if i == max(1, stages - 3):
+            play()
+        if i == max(1, stages - 2):
+            answers_on()
 
     head_step(stages - 1)
+    for i in range(stages):
+        for way in (0, 1):
+            head_come(way, 1, i).wait_recv()
     head_final[side] = jnp.sum(head_all[...].astype(F32), 0)
     hlast = remote(head_final.at[side], head_final.at[side], hlast_send, hlast_recv, sibling)
     hlast.start()
 
-    def played_come(i):
-        return remote(
-            played_out.at[to_agent[i]], played_in.at[from_agent[i]], played_send.at[i], played_recv.at[i], (to_agent[i], dp)
-        )
-
-    for i in range(len(shifts)):
-        played_come(i).wait_recv()
+    for i in range(agent_x - 1):
+        answers_x(i, x_from[i]).wait_recv()
     back = played_in[...].astype(F32).reshape(agents * SLOTS, PAD).T.astype(BF16)
     opp_out[...] = dot(back, placed)[:32].astype(BF16)
 
@@ -460,9 +490,12 @@
     hlast.wait_send()
     for f in range(CHUNKS):
         swap(f).wait_send()
-    for i in range(len(shifts)):
-        send_frames(i).wait_send()
-        played_come(i).wait_send()
+    for i in range(agent_x - 1):
+        frames_x(i, ax).wait_send()
+        answers_x(i, ax).wait_send()
+    for i in range(agent_y - 1):
+        frames_y(i, ay).wait_send()
+        answers_y(i, ay).wait_send()
 
 
 def adam_step(master, moment, second, grad, rate):
@@ -500,17 +533,16 @@
     agent_y = 4 if agents % 4 == 0 else agents
     sizes = (agents, chips, shard, envs, steps, feat, units, head_rows, agent_y)
     vmem, dma = pltpu.VMEM, pltpu.SemaphoreType.DMA
-    shifts = max(1, agents - 1)
     anywhere = pl.BlockSpec(memory_space=pl.ANY)
     in_vmem = pl.BlockSpec(memory_space=vmem)
     head_rows_first = [a.swapaxes(0, 1) for a in (head_master, head_mom, head_vel)]
     grad, head_grad, own_net, opp_net = pl.pallas_call(
         functools.partial(step_kernel, sizes),
         out_shape=(
-            jax.ShapeDtypeStruct((shard, width), F32),
-            jax.ShapeDtypeStruct((2, 32, units // 2), F32),
-            jax.ShapeDtypeStruct((32, envs), F32),
-            jax.ShapeDtypeStruct((32, envs), BF16),
+            vmem((shard, width), F32),
+            vmem((2, 32, units // 2), F32),
+            vmem((32, envs), F32),
+            vmem((32, envs), BF16),
         ),
         in_specs=[anywhere] * 10,
         out_specs=(in_vmem,) * 4,
@@ -532,10 +564,12 @@
             vmem((chips, shard, width), BF16),
             vmem((2, 2, stages, shard, width), BF16),
             vmem((2, 2, stages, shard, width), BF16),
-            vmem((agents, SLOTS, feat), BF16),
-            vmem((agents, SLOTS, feat), BF16),
-            vmem((agents, SLOTS, PAD), BF16),
-            vmem((agents, SLOTS, PAD), BF16),
+            vmem((agents // agent_y, agent_y, SLOTS, feat), BF16),
+            vmem((agents // agent_y, agent_y, SLOTS, feat), BF16),
+            vmem((agents // agent_y, agent_y, SLOTS, feat), BF16),
+            vmem((agents // agent_y, agent_y, SLOTS, PAD), BF16),
+            vmem((agents // agent_y, agent_y, SLOTS, PAD), BF16),
+            vmem((agents // agent_y, agent_y, SLOTS, PAD), BF16),
             vmem((PAD, units), F32),
             vmem((2, 32, units // 2), BF16),
             vmem((32, units // 2), BF16),
@@ -548,10 +582,10 @@
             dma((2, 2, stages, CHUNKS)),
             dma,
             dma,
-            dma((shifts,)),
-            dma((shifts,)),
-            dma((shifts,)),
-            dma((shifts,)),
+            dma((2, agent_y)),
+            dma((2, agent_y)),
+            dma((2, agent_y)),
+            dma((2, agent_y)),
             dma((2, 2, stages, CHUNKS)),
             dma((2, 2, stages, CHUNKS)),
             dma((CHUNKS,)),

time: 70.3 us -> 62.8 us (0.89)
  the two profiles are of different devices: /device:TPU:1 before, /device:TPU:6 now
where the time goes in v3:
time: 62.8 us; the launch traced here: 62.6 us
  Pallas kernels  61.1 us (97%)
  between operations  1.47 us (2%)
    pallas_call x1, Pallas kernels, per_device(): pl.pallas_call(functools.partial(step_kernel, sizes), out_shape=(vmem((sh...  60.3 us

profile of v3, /device:TPU:6, one launch (start us, length us, event | category | flops | bytes accessed | tf_op | source)
XLA Modules:
  0.0 62.6 jit_solution(11064880470133974943)
XLA Ops:
  0.6 0.0 copy-start
  0.6 0.0 copy-start.5
  0.7 0.0 copy-start.4
  0.7 0.0 copy-start.3
  0.7 0.0 copy-start.2
  0.7 0.0 copy-start.1
  1.4 60.3 %shard_map.206 = (f32[8,3712]{1,0:T(8,128)S(1)}, f32[2,32,128]{2,1,0:T(8,128)S(1)}, f32[32,32]{1,0:T(8,128)S(1)}, bf16[32,32]{1,0:T(8,128)(2,1)S(1)}) custom-call(bf16[1,32,16,3456]{3,2,1,0:T(8,128)(2,1)} %learn_hbm.1, bf16[1,32,3456]{2,1,0:T(8,128)(2,1)} %own_hbm.1, bf16[1,32,3456]{2,1,0:T(8,128)(2,1)} %opp_hbm.1, s32[1,1,32]{2,1,0:T(1,128)} %bitcast.21, ...), custom_call_target="tpu_custom_call" | custom-call | tf_op jit(solution)/shard_map/pallas_call | solution.py:539
  61.7 0.0 copy-done
  61.7 0.0 copy-done.5
  61.7 0.0 copy-done.4
  61.7 0.0 copy-done.3
  61.8 0.0 copy-done.2
  61.8 0.0 copy-done.1
  61.8 0.8 %shard_map.207 = (f32[18,1,32]{2,1,0:T(1,128)}, bf16[1,18,32]{2,1,0:T(8,128)(2,1)}, f32[1,8,3712]{2,1,0:T(8,128)}, f32[1,8,3712]{2,1,0:T(8,128)}, f32[1,8,3712]{...) custom-call(f32[1]{0:T(128)S(6)} %copy.23.rate, ...), custom_call_target="tpu_custom_call" | custom-call | tf_op jit(solution)/shard_map/pallas_call | solution.py:607
Async XLA Ops:
  0.6 61.1 %copy-start = (f32[1,8,3712]{2,1,0:T(8,128)S(1)}, f32[1,8,3712]{2,1,0:T(8,128)}, u32[]{:S(2)}) copy-start(f32[1,8,3712]{2,1,0:T(8,128)} %core.1) | copy-start | bytes 356356
  0.6 61.1 %copy-start.5 = (f32[1,19,256]{2,0,1:T(1,128)S(1)}, f32[1,19,256]{2,0,1:T(1,128)}, u32[]{:S(2)}) copy-start(f32[1,19,256]{2,0,1:T(1,128)} %param.28) | copy-start | bytes 58372
  0.7 61.1 %copy-start.4 = (f32[1,19,256]{2,0,1:T(1,128)S(1)}, f32[1,19,256]{2,0,1:T(1,128)}, u32[]{:S(2)}) copy-start(f32[1,19,256]{2,0,1:T(1,128)} %param.27) | copy-start | bytes 58372
  0.7 61.1 %copy-start.3 = (f32[1,19,256]{2,0,1:T(1,128)S(1)}, f32[1,19,256]{2,0,1:T(1,128)}, u32[]{:S(2)}) copy-start(f32[1,19,256]{2,0,1:T(1,128)} %param.26) | copy-start | bytes 58372
  0.7 61.1 %copy-start.2 = (f32[1,8,3712]{2,1,0:T(8,128)S(1)}, f32[1,8,3712]{2,1,0:T(8,128)}, u32[]{:S(2)}) copy-start(f32[1,8,3712]{2,1,0:T(8,128)} %core_vel.1) | copy-start | bytes 356356
  0.7 61.1 %copy-start.1 = (f32[1,8,3712]{2,1,0:T(8,128)S(1)}, f32[1,8,3712]{2,1,0:T(8,128)}, u32[]{:S(2)}) copy-start(f32[1,8,3712]{2,1,0:T(8,128)} %core_mom.1) | copy-start | bytes 356356

commit v4 on v3

--- a/solution.py
+++ b/solution.py
@@ -362,6 +362,39 @@
             for_sibling.at[:, :, cols(f)], from_sibling.at[:, :, cols(f)], half_send.at[f], half_recv.at[f], sibling
         )
 
+    def reduce_has(way, kind, i, f):
+        return kind == 1 or i > 0 or (f < half) == (way == 0)
+
+    def reduce_to(way, kind, i, f):
+        at = (way, kind, i)
+        return remote(
+            sums_out.at[(*at, slice(None), cols(f))], sums_in.at[(*at, slice(None), cols(f))],
+            reduce_send.at[(*at, f)], reduce_recv.at[(*at, f)], target[kind][way],
+        )
+
+    def arrived(way, i, f, term):
+        for kind in kinds:
+            if reduce_has(way, kind, i, f):
+                reduce_to(way, kind, i, f).wait_recv()
+                term = term + sums_in[way, kind, i, :, cols(f)].astype(F32)
+        return term
+
+    def reduce_step(way, i, f):
+        for kind in kinds:
+            if reduce_has(way, kind, i, f):
+                term = mine[chip_at(sign[way] * (far - 2 * i - kind)), :, cols(f)]
+                if kind == 0 and i > 0:
+                    term = arrived(way, i - 1, f, term)
+                sums_out[way, kind, i, :, cols(f)] = term.astype(BF16)
+                reduce_to(way, kind, i, f).start()
+
+    def first_stage(f):
+        swap(f).wait_recv()
+        lo, hi = edges[f], edges[f + 1]
+        mine[:, :, lo:hi] = mine[:, :, lo:hi] + from_sibling[:, :, lo:hi].astype(F32)
+        for way in (0, 1):
+            reduce_step(way, 0, f)
+
     first_side = side == 0
     for f in range(CHUNKS):
         lo, hi = edges[f], edges[f + 1]
@@ -375,39 +408,9 @@
         for_sibling[:, :, lo:hi] = jnp.where(first_side, grad[:, 1], grad[:, 0]).astype(BF16)
         swap(f).start()
         mine[:, :, lo:hi] = jnp.where(first_side, grad[:, 0], grad[:, 1])
-
-    def reduce_has(way, kind, i, f):
-        return kind == 1 or i > 0 or (f < half) == (way == 0)
-
-    def reduce_to(way, kind, i, f):
-        at = (way, kind, i)
-        return remote(
-            sums_out.at[(*at, slice(None), cols(f))], sums_in.at[(*at, slice(None), cols(f))],
-            reduce_send.at[(*at, f)], reduce_recv.at[(*at, f)], target[kind][way],
-        )
-
-    def arrived(way, i, f, term):
-        for kind in kinds:
-            if reduce_has(way, kind, i, f):
-                reduce_to(way, kind, i, f).wait_recv()
-                term = term + sums_in[way, kind, i, :, cols(f)].astype(F32)
-        return term
-
-    def reduce_step(way, i, f):
-        for kind in kinds:
-            if reduce_has(way, kind, i, f):
-                term = mine[chip_at(sign[way] * (far - 2 * i - kind)), :, cols(f)]
-                if kind == 0 and i > 0:
-                    term = arrived(way, i - 1, f, term)
-                sums_out[way, kind, i, :, cols(f)] = term.astype(BF16)
-                reduce_to(way, kind, i, f).start()
-
-    for f in range(CHUNKS):
-        swap(f).wait_recv()
-        lo, hi = edges[f], edges[f + 1]
-        mine[:, :, lo:hi] = mine[:, :, lo:hi] + from_sibling[:, :, lo:hi].astype(F32)
-        for way in (0, 1):
-            reduce_step(way, 0, f)
+        if f > 0:
+            first_stage(f - 1)
+    first_stage(CHUNKS - 1)
 
     def answers_y(i, at):
         return remote(

time: 62.8 us -> 62.4 us (level)
  the two profiles are of different devices: /device:TPU:6 before, /device:TPU:1 now
where the time goes in v4:
time: 62.4 us; the launch traced here: 61.4 us
  Pallas kernels  59.9 us (96%)
  between operations  1.47 us (2%)
    pallas_call x1, Pallas kernels, per_device(): pl.pallas_call(functools.partial(step_kernel, sizes), out_shape=(vmem((sh...  59.1 us

profile of v4, /device:TPU:1, one launch (start us, length us, event | category | flops | bytes accessed | tf_op | source)
XLA Modules:
  0.0 61.4 jit_solution(13026127489723317755)
XLA Ops:
  0.6 0.0 copy-start
  0.6 0.0 copy-start.5
  0.7 0.0 copy-start.4
  0.7 0.0 copy-start.3
  0.7 0.0 copy-start.2
  0.7 0.0 copy-start.1
  1.4 59.1 %shard_map.206 = (f32[8,3712]{1,0:T(8,128)S(1)}, f32[2,32,128]{2,1,0:T(8,128)S(1)}, f32[32,32]{1,0:T(8,128)S(1)}, bf16[32,32]{1,0:T(8,128)(2,1)S(1)}) custom-call(bf16[1,32,16,3456]{3,2,1,0:T(8,128)(2,1)} %learn_hbm.1, bf16[1,32,3456]{2,1,0:T(8,128)(2,1)} %own_hbm.1, bf16[1,32,3456]{2,1,0:T(8,128)(2,1)} %opp_hbm.1, s32[1,1,32]{2,1,0:T(1,128)} %bitcast.21, ...), custom_call_target="tpu_custom_call" | custom-call | tf_op jit(solution)/shard_map/pallas_call | solution.py:542
  60.5 0.0 copy-done
  60.5 0.0 copy-done.5
  60.5 0.0 copy-done.4
  60.5 0.0 copy-done.3
  60.5 0.0 copy-done.2
  60.6 0.0 copy-done.1
  60.6 0.8 %shard_map.207 = (f32[18,1,32]{2,1,0:T(1,128)}, bf16[1,18,32]{2,1,0:T(8,128)(2,1)}, f32[1,8,3712]{2,1,0:T(8,128)}, f32[1,8,3712]{2,1,0:T(8,128)}, f32[1,8,3712]{...) custom-call(f32[1]{0:T(128)S(6)} %copy.23.rate, ...), custom_call_target="tpu_custom_call" | custom-call | tf_op jit(solution)/shard_map/pallas_call | solution.py:610
Async XLA Ops:
  0.6 59.9 %copy-start = (f32[1,8,3712]{2,1,0:T(8,128)S(1)}, f32[1,8,3712]{2,1,0:T(8,128)}, u32[]{:S(2)}) copy-start(f32[1,8,3712]{2,1,0:T(8,128)} %core.1) | copy-start | bytes 356356
  0.6 59.9 %copy-start.5 = (f32[1,19,256]{2,0,1:T(1,128)S(1)}, f32[1,19,256]{2,0,1:T(1,128)}, u32[]{:S(2)}) copy-start(f32[1,19,256]{2,0,1:T(1,128)} %param.28) | copy-start | bytes 58372
  0.7 59.9 %copy-start.4 = (f32[1,19,256]{2,0,1:T(1,128)S(1)}, f32[1,19,256]{2,0,1:T(1,128)}, u32[]{:S(2)}) copy-start(f32[1,19,256]{2,0,1:T(1,128)} %param.27) | copy-start | bytes 58372
  0.7 59.9 %copy-start.3 = (f32[1,19,256]{2,0,1:T(1,128)S(1)}, f32[1,19,256]{2,0,1:T(1,128)}, u32[]{:S(2)}) copy-start(f32[1,19,256]{2,0,1:T(1,128)} %param.26) | copy-start | bytes 58372
  0.7 59.9 %copy-start.2 = (f32[1,8,3712]{2,1,0:T(8,128)S(1)}, f32[1,8,3712]{2,1,0:T(8,128)}, u32[]{:S(2)}) copy-start(f32[1,8,3712]{2,1,0:T(8,128)} %core_vel.1) | copy-start | bytes 356356
  0.7 59.9 %copy-start.1 = (f32[1,8,3712]{2,1,0:T(8,128)S(1)}, f32[1,8,3712]{2,1,0:T(8,128)}, u32[]{:S(2)}) copy-start(f32[1,8,3712]{2,1,0:T(8,128)} %core_mom.1) | copy-start | bytes 356356
